TPU v7x, 32 devices: a whole 2x2x4 slice. The times are simulated.
32 devices in a mesh: gx: 4 (over x, core), gy: 4 (over z), gz: 2 (over y).
Axes of the slice: x: 2, y: 2, z: 4, core: 2. Of those that a mesh axis runs over, the one named last changes fastest.
Arguments:
- e_field: float32 [3, 32, 64, 256], P(None, 'gx', 'gy', 'gz'), may hold values from -6 to 6
- h_field: float32 [3, 32, 64, 256], P(None, 'gx', 'gy', 'gz'), may hold values from -6 to 6
- permittivity: float32 [32, 64, 256], P('gx', 'gy', 'gz'), may hold values from 1 to 4
- wall_mask: int32 [32, 64, 256], P('gx', 'gy', 'gz'), may hold values 0 or 1
- poles: float32 [8, 3, 32, 64, 256], P(None, None, 'gx', 'gy', 'gz'), may hold values from -4 to 4
- pole_decay: float32 [8], replicated, may hold values from 0.2 to 0.95
- pole_gain: float32 [8], replicated, may hold values from 0.05 to 0.3
- face_cells: int32 [1024], P(('gx', 'gy', 'gz')), may hold values from 0 to 16383
- owners: int32 [1024, 1], P(('gx', 'gy', 'gz')), may hold values from 0 to 3; in each aligned block of 32 rows (0 to 31, 32 to 63, ...) at most 16 rows name the same one
- history: bfloat16 [63, 4, 1024], P(None, None, ('gx', 'gy', 'gz')), may hold values from -6 to 6
- steering: bfloat16 [4, 2048, 4096], P(None, ('gx', 'gy'), 'gz'), may hold values from -0.09375 to 0.09375
Outputs:
- e_next: float32 [3, 32, 64, 256], P(None, 'gx', 'gy', 'gz')
- h_next: float32 [3, 32, 64, 256], P(None, 'gx', 'gy', 'gz')
- poles_next: float32 [8, 3, 32, 64, 256], P(None, None, 'gx', 'gy', 'gz')
- far_field: float32 [2, 256, 4096], P(None, ('gx', 'gy'), 'gz')
Inputs may be any that keep to these rules, and one draw needn't show every extreme that they name: `face_cells`: index of the sample's cell within its device's block, row-major over 8 x 16 x 128. `owners`: among the samples of one device at most 16 name the same owner, and some device has exactly 16 for one owner.
All inputs are finite; a program needn't handle non-finite values. No bound on the sum of `wall_mask` on one device may be relied on, other than what follows from the above.
Results may differ from a plain program's by a relative error of at most 0.00063.
Values may be sent and summed in bfloat16 or wider, within the bound.
A program may use at most 64 MiB of HBM per device.

v0:
```python
import math

import jax
import jax.numpy as jnp
from jax import lax
from jax.sharding import PartitionSpec as P

FREQS = 256


def padded_2(block, sides, width):
    for axis, dim in sides:
        count = lax.axis_size(axis)
        forward = [(i, i + 1) for i in range(count - 1)]
        backward = [(target, source) for source, target in forward]
        low = lax.ppermute(
            lax.slice_in_dim(block, block.shape[dim] - width, None, axis=dim), axis, forward
        )
        high = lax.ppermute(lax.slice_in_dim(block, 0, width, axis=dim), axis, backward)
        block = jnp.concatenate([low, block, high], axis=dim)
    return block


def window(field, shift_x, shift_y, shift_z, span_x, span_y, span_z):
    return lax.slice(
        field, (shift_x, shift_y, shift_z), (shift_x + span_x, shift_y + span_y, shift_z + span_z)
    )


def spectral_rows(count, freqs, steps):
    times = jnp.arange(steps, dtype=jnp.float32)
    levels = jnp.arange(count, dtype=jnp.float32) + 0.5
    phase = math.pi / (2.0 * freqs) * levels[:, None] * times[None, :]
    scale = 1.0 / math.sqrt(steps)
    return jnp.stack([jnp.cos(phase) * scale, -jnp.sin(phase) * scale])


def bucket_rank(owner, groups):
    onehot = (owner[..., None] == jnp.arange(groups, dtype=jnp.int32)).astype(jnp.int32)
    return jnp.sum((jnp.cumsum(onehot, axis=-2) - onehot) * onehot, axis=-1)


def project(tile_rows, weights, steps):
    currents = tile_rows.reshape(tile_rows.shape[0], steps, 4)
    return jnp.einsum("rtc,crd->td", currents, weights, preferred_element_type=jnp.float32)


def fields_both(e_field, h_field):
    span_x, span_y, span_z = (e_field.shape[1], e_field.shape[2], e_field.shape[3])
    both = jnp.concatenate([e_field, h_field], axis=0)
    padded = padded_2(both, (("gx", 1), ("gy", 2), ("gz", 3)), 1)
    ext_x, ext_y, ext_z = (span_x + 1, span_y + 1, span_z + 1)

    def upper(comp, shift_x, shift_y, shift_z):
        return window(padded[comp], shift_x, shift_y, shift_z, ext_x, ext_y, ext_z)

    mag_x = upper(3, 0, 0, 0) - 0.5 * (
        upper(2, 0, 1, 0) - upper(2, 0, 0, 0) - (upper(1, 0, 0, 1) - upper(1, 0, 0, 0))
    )
    mag_y = upper(4, 0, 0, 0) - 0.5 * (
        upper(0, 0, 0, 1) - upper(0, 0, 0, 0) - (upper(2, 1, 0, 0) - upper(2, 0, 0, 0))
    )
    mag_z = upper(5, 0, 0, 0) - 0.5 * (
        upper(1, 1, 0, 0) - upper(1, 0, 0, 0) - (upper(0, 0, 1, 0) - upper(0, 0, 0, 0))
    )
    keep_x = (jnp.arange(ext_x) > 0) | (lax.axis_index("gx") > 0)
    keep_y = (jnp.arange(ext_y) > 0) | (lax.axis_index("gy") > 0)
    keep_z = (jnp.arange(ext_z) > 0) | (lax.axis_index("gz") > 0)
    keep = keep_x[:, None, None] & keep_y[None, :, None] & keep_z[None, None, :]
    magnetic = jnp.where(keep[None], jnp.stack([mag_x, mag_y, mag_z]), 0.0)

    def lower(comp, back_x, back_y, back_z):
        return window(magnetic[comp], 1 - back_x, 1 - back_y, 1 - back_z, span_x, span_y, span_z)

    drive = jnp.stack(
        [
            lower(2, 0, 0, 0) - lower(2, 0, 1, 0) - (lower(1, 0, 0, 0) - lower(1, 0, 0, 1)),
            lower(0, 0, 0, 0) - lower(0, 0, 0, 1) - (lower(2, 0, 0, 0) - lower(2, 1, 0, 0)),
            lower(1, 0, 0, 0) - lower(1, 1, 0, 0) - (lower(0, 0, 0, 0) - lower(0, 0, 1, 0)),
        ]
    )
    return (magnetic[:, 1:, 1:, 1:], drive)


def per_device(
    e_field,
    h_field,
    permittivity,
    wall_mask,
    poles,
    pole_decay,
    pole_gain,
    face_cells,
    owners,
    history,
    steering,
):
    h_next, drive = fields_both(e_field, h_field)
    poles_next = (
        pole_decay[:, None, None, None, None] * poles
        + pole_gain[:, None, None, None, None] * drive[None]
    )
    e_next = jnp.where(
        wall_mask[None] == 1,
        jnp.sum(poles_next, axis=0),
        e_field + (0.5 / permittivity)[None] * drive,
    )
    count = face_cells.shape[0]
    steps = history.shape[0] + 1
    picked = jnp.stack([e_next[0], e_next[1], h_next[0], h_next[1]]).reshape(4, -1)
    fresh = jnp.take(picked, face_cells, axis=1).astype(jnp.bfloat16)
    series = jnp.concatenate([history, fresh[None]], axis=0)
    sample_rows = jnp.transpose(series, (2, 0, 1)).reshape(count, steps * 4)
    owner = owners[:, 0]
    groups = lax.axis_size("gx")
    depth = lax.axis_size("gz")
    capacity = 2 * count // groups
    tile = steering.shape[1]
    every_rows, every_owner = (
        lax.all_gather(sample_rows, ("gx", "gz"), axis=0, tiled=True),
        lax.all_gather(owner[:, None], ("gx", "gz"), axis=0, tiled=True),
    )
    owner_all = every_owner[:, 0].reshape(groups * depth, count)
    rank_all = bucket_rank(owner_all, groups)
    block_ids = jnp.arange(groups * depth, dtype=jnp.int32)
    source_x = block_ids // depth
    source_z = block_ids % depth
    target = source_z[:, None] * (groups * capacity) + source_x[:, None] * capacity + rank_all
    target = jnp.where(owner_all == lax.axis_index("gx"), target, -1).reshape(-1)
    select = (target[:, None] == jnp.arange(tile, dtype=jnp.int32)[None, :]).astype(jnp.bfloat16)
    tile_rows = jnp.einsum(
        "ks,kw->sw", select, every_rows, preferred_element_type=jnp.float32
    ).astype(jnp.bfloat16)
    projected = project(tile_rows, steering, steps)
    shared = lax.psum_scatter(projected, ("gx", "gy"), scatter_dimension=1, tiled=True)
    table = spectral_rows(FREQS, FREQS, steps)
    spectra = jnp.einsum("sft,td->sfd", table, shared, precision=lax.Precision.HIGHEST)
    far_field = lax.all_to_all(spectra, ("gx", "gy"), split_axis=1, concat_axis=2, tiled=True)
    return (e_next, h_next, poles_next, far_field)


def solution(mesh):
    return jax.shard_map(
        per_device,
        mesh=mesh,
        in_specs=(
            P(None, "gx", "gy", "gz"),
            P(None, "gx", "gy", "gz"),
            P("gx", "gy", "gz"),
            P("gx", "gy", "gz"),
            P(None, None, "gx", "gy", "gz"),
            P(),
            P(),
            P(("gx", "gy", "gz")),
            P(("gx", "gy", "gz"), None),
            P(None, None, ("gx", "gy", "gz")),
            P(None, ("gx", "gy"), "gz"),
        ),
        out_specs=(
            P(None, "gx", "gy", "gz"),
            P(None, "gx", "gy", "gz"),
            P(None, None, "gx", "gy", "gz"),
            P(None, ("gx", "gy"), "gz"),
        ),
        check_vma=False,
    )
```

profile of v0, /device:TPU:0, one launch (start us, length us, event | category | flops | bytes accessed | tf_op | source)
XLA Modules:
  0.0 163.2 jit_solution(3078176266176776995)
XLA Ops:
  7.2 1.1 constant_dynamic-update-slice_fusion.1
  9.3 1.3 collective-permute-start.1
  10.6 3.0 %collective-permute-start = (f32[6,1,16,128]{3,2,1,0:T(8,128)S(1)}, f32[6,1,16,128]{3,2,1,0:T(8,128)S(1)}, u32[]{:S(2)}, u32[]{:S(2)}) collective-permute-start(f32[6,1,16,128]{3,2,1,0:T(8,128)S(1)} %get-tuple-element.27), channel_id=1, source_target_pairs={{0,8},{8,16},{16,24},{1,9},{9,17},{17,25},{2,10},{10,18},{18,26},{... | collective-permute-start | bytes 147464 | tf_op jit(solution)/shard_map/ppermute | solution.py:16
  13.7 1.2 dynamic-slice
  16.3 8.8 %all-reduce = s32[256]{0:T(256)S(1)} all-reduce(s32[256]{0:T(256)S(1)} %bitcast_dynamic-update-slice_fusion), channel_id=1, replica_groups=mesh['gx'=4,'gy'=4,'gz'=2] {'gx','gz'}, use_global_device_ids=true, to_apply=%add | all-reduce | flops 256 | bytes 2048
  28.9 1.3 collective-permute-start.3
  30.2 4.5 %collective-permute-start.2 = (f32[6,10,1,128]{3,2,1,0:T(1,128)S(1)}, f32[6,10,1,128]{3,2,1,0:T(1,128)S(1)}, u32[]{:S(2)}, u32[]{:S(2)}) collective-permute-start(f32[6,10,1,128]{3,2,1,0:T(1,128)S(1)} %get-tuple-element.25), channel_id=1, source_target_pairs={{0,2},{2,4},{4,6},{1,3},{3,5},{5,7},{8,10},{10,12},{12,14},{9,11},... | collective-permute-start | bytes 92168 | tf_op jit(solution)/shard_map/ppermute | solution.py:16
  34.8 1.5 collective-permute-done.2
  36.5 1.1 fusion.34
  37.5 2.2 %copy.117 = f32[6,10,18,1]{2,3,1,0:T(1,128)} copy(f32[6,10,18,1]{3,2,1,0:T(8,128)} %get-tuple-element.21) | data formatting | bytes 8640
  39.7 1.3 collective-permute-start.5
  42.1 5.7 %collective-permute-start.4 = (f32[6,10,18,1]{2,3,1,0:T(1,128)}, f32[6,10,18,1]{2,3,1,0:T(1,128)}, u32[]{:S(2)}, u32[]{:S(2)}) collective-permute-start(f32[6,10,18,1]{2,3,1,0:T(1,128)} %copy.116), channel_id=1, source_target_pairs={{0,1},{2,3},{4,5},{6,7},{8,9},{10,11},{12,13},{14,15},{16,17},{18,... | collective-permute-start | bytes 12968 | tf_op jit(solution)/shard_map/ppermute | solution.py:16
  47.8 1.2 copy.104
  49.0 2.1 %copy.103 = f32[6,10,18,1]{3,2,1,0:T(8,128)} copy(f32[6,10,18,1]{2,3,1,0:T(1,128)} %collective-permute-done.4) | data formatting | bytes 8640 | tf_op jit(solution)/shard_map/ppermute | solution.py:16
  51.1 2.0 %pad_maximum_fusion = f32[6,10,18,130]{3,2,1,0:T(8,128)S(1)} fusion(f32[6,10,18,1]{3,2,1,0:T(8,128)S(1)} %copy.104, f32[6,10,1,128]{3,2,1,0:T(1,128)S(1)} %collective-permute-done.3, f32[6,1,16,128]{3,2,1,0:T(8,128)S(1)} %collective-permute-done.1, f32[6,8,16,128]{3,2,1,0:T(8,128)S(1)} %constant_dynamic-update-slice_fusion, ...), kind=kLoop, calls=%fused_computation.3 | loop fusion | flops 842400 | bytes 1123200 | tf_op jit(solution)/shard_map/concatenate | solution.py:20
  55.0 1.4 fusion.33
  56.5 3.3 %copy.107 = bf16[4,8,16,128]{0,3,2,1:T(8,128)(2,1)} copy(bf16[4,8,16,128]{3,2,1,0:T(8,128)(2,1)S(1)} %pad_maximum_fusion.2) | data formatting | bytes 262144 | tf_op jit(solution)/shard_map/stack | solution.py:110
  59.8 3.3 %gather_fusion = bf16[32,4]{1,0:T(8,128)(2,1)S(1)} fusion(bf16[4,16384]{0,1:T(8,128)(2,1)} %bitcast.56, s32[1024]{0:T(1024)S(1)} %pad_clamp_fusion), kind=kCustom, calls=%fused_computation | custom fusion | bytes 640 | tf_op jit(solution)/shard_map/jit(_take)/gather | solution.py:111
  63.7 16.7 %all_gather.7 = bf16[256,256]{1,0:T(8,128)(2,1)S(1)} all-gather(bf16[32,256]{1,0:T(8,128)(2,1)S(1)} %copy.111), channel_id=1, replica_groups=mesh['gx'=4,'gy'=4,'gz'=2] {'gx','gz'}, dimensions={0}, use_global_device_ids=true | all-gather | bytes 147456 | tf_op jit(solution)/shard_map/all_gather | solution.py:120
  80.8 1.3 convolution_bitcast_fusion
  82.4 57.0 %reduce-scatter.2.cloned.1.call-done = f32[64,128]{1,0:T(8,128)} async-done(((f32[64,2048]{1,0:T(8,128)}), f32[64,128]{1,0:T(8,128)}) %reduce-scatter.2.cloned.1.call-update) | async-done | bytes 32784 | tf_op jit(solution)/shard_map/reduce_scatter | solution.py:135
  139.4 1.4 fusion.13
  141.7 3.7 %all-to-all-start = ((f32[2,256,128]{2,0,1:T(2,128)}), f32[2,256,128]{2,0,1:T(2,128)S(1)}, u32[]{:S(2)}, u32[]{:S(2)}) async-start(f32[2,256,128]{2,0,1:T(2,128)} %copy.114), calls=%async_computation.1 | async-start | bytes 524288 | tf_op jit(solution)/shard_map/all_to_all | solution.py:138
  146.2 9.3 %all-to-all-done = f32[2,256,128]{2,0,1:T(2,128)S(1)} async-done(((f32[2,256,128]{2,0,1:T(2,128)}), f32[2,256,128]{2,0,1:T(2,128)S(1)}, u32[]{:S(2)}, u32[]{:S(2)}) %all-to-all-start) | async-done | bytes 262176 | tf_op jit(solution)/shard_map/all_to_all | solution.py:138
  (73 shorter events, 12.4 us)
Async XLA Ops:
  7.2 73.6 %copy-start = (bf16[4,128,2048]{2,1,0:T(8,128)(2,1)S(1)}, bf16[4,128,2048]{2,1,0:T(8,128)(2,1)}, u32[]{:S(2)}) copy-start(bf16[4,128,2048]{2,1,0:T(8,128)(2,1)} %param.21) | copy-start | bytes 6291460
  7.2 27.6 %copy-start.7 = (s32[32]{0:T(128)S(1)}, s32[32]{0:T(128)}, u32[]{:S(2)}) copy-start(s32[32]{0:T(128)} %param.18) | copy-start | bytes 388
  7.2 132.2 %reduce-scatter.2.cloned.1.call-start = ((), (), s32[]{:S(2)}) async-start(), calls=%async_computation.2 | async-start | bytes 557056 | tf_op jit(solution)/shard_map/reduce_scatter | solution.py:135
  9.3 19.6 %collective-permute-start.1 = (f32[6,1,16,128]{3,2,1,0:T(8,128)S(1)}, f32[6,1,16,128]{3,2,1,0:T(8,128)S(1)}, u32[]{:S(2)}, u32[]{:S(2)}) collective-permute-start(f32[6,1,16,128]{3,2,1,0:T(8,128)S(1)} %get-tuple-element.28), channel_id=1, source_target_pairs={{8,0},{16,8},{24,16},{9,1},{17,9},{25,17},{10,2},{18,10},{26,18},{... | collective-permute-start | bytes 147464 | tf_op jit(solution)/shard_map/ppermute | solution.py:19
  10.6 18.3 %collective-permute-start = (f32[6,1,16,128]{3,2,1,0:T(8,128)S(1)}, f32[6,1,16,128]{3,2,1,0:T(8,128)S(1)}, u32[]{:S(2)}, u32[]{:S(2)}) collective-permute-start(f32[6,1,16,128]{3,2,1,0:T(8,128)S(1)} %get-tuple-element.27), channel_id=1, source_target_pairs={{0,8},{8,16},{16,24},{1,9},{9,17},{17,25},{2,10},{10,18},{18,26},{... | collective-permute-start | bytes 147464 | tf_op jit(solution)/shard_map/ppermute | solution.py:16
  28.9 5.9 %collective-permute-start.3 = (f32[6,10,1,128]{3,2,1,0:T(1,128)S(1)}, f32[6,10,1,128]{3,2,1,0:T(1,128)S(1)}, u32[]{:S(2)}, u32[]{:S(2)}) collective-permute-start(f32[6,10,1,128]{3,2,1,0:T(1,128)S(1)} %get-tuple-element.26), channel_id=1, source_target_pairs={{2,0},{4,2},{6,4},{3,1},{5,3},{7,5},{10,8},{12,10},{14,12},{11,9},... | collective-permute-start | bytes 92168 | tf_op jit(solution)/shard_map/ppermute | solution.py:19
  30.2 6.1 %collective-permute-start.2 = (f32[6,10,1,128]{3,2,1,0:T(1,128)S(1)}, f32[6,10,1,128]{3,2,1,0:T(1,128)S(1)}, u32[]{:S(2)}, u32[]{:S(2)}) collective-permute-start(f32[6,10,1,128]{3,2,1,0:T(1,128)S(1)} %get-tuple-element.25), channel_id=1, source_target_pairs={{0,2},{2,4},{4,6},{1,3},{3,5},{5,7},{8,10},{10,12},{12,14},{9,11},... | collective-permute-start | bytes 92168 | tf_op jit(solution)/shard_map/ppermute | solution.py:16
  39.7 8.1 %collective-permute-start.5 = (f32[6,10,18,1]{2,3,1,0:T(1,128)}, f32[6,10,18,1]{2,3,1,0:T(1,128)}, u32[]{:S(2)}, u32[]{:S(2)}) collective-permute-start(f32[6,10,18,1]{2,3,1,0:T(1,128)} %copy.117), channel_id=1, source_target_pairs={{1,0},{3,2},{5,4},{7,6},{9,8},{11,10},{13,12},{15,14},{17,16},{19,... | collective-permute-start | bytes 12968 | tf_op jit(solution)/shard_map/ppermute | solution.py:19
  42.1 7.0 %collective-permute-start.4 = (f32[6,10,18,1]{2,3,1,0:T(1,128)}, f32[6,10,18,1]{2,3,1,0:T(1,128)}, u32[]{:S(2)}, u32[]{:S(2)}) collective-permute-start(f32[6,10,18,1]{2,3,1,0:T(1,128)} %copy.116), channel_id=1, source_target_pairs={{0,1},{2,3},{4,5},{6,7},{8,9},{10,11},{12,13},{14,15},{16,17},{18,... | collective-permute-start | bytes 12968 | tf_op jit(solution)/shard_map/ppermute | solution.py:16
  53.6 1.4 copy-start.1
  53.6 1.4 copy-start.5
  53.6 1.4 copy-start.6
  55.0 1.4 copy-start.2
  56.5 3.4 %copy-start.3 = (f32[3,8,16,128]{3,2,1,0:T(8,128)}, f32[3,8,16,128]{3,2,1,0:T(8,128)S(1)}, u32[]{:S(2)}) copy-start(f32[3,8,16,128]{3,2,1,0:T(8,128)S(1)} %add_select_fusion) | copy-start | bytes 589828
  56.5 6.8 %copy-start.4 = (bf16[63,4,32]{0,2,1:T(8,128)(2,1)S(1)}, bf16[63,4,32]{0,2,1:T(8,128)(2,1)}, u32[]{:S(2)}) copy-start(bf16[63,4,32]{0,2,1:T(8,128)(2,1)} %param.20) | copy-start | bytes 48388
  141.7 13.8 %all-to-all-start = ((f32[2,256,128]{2,0,1:T(2,128)}), f32[2,256,128]{2,0,1:T(2,128)S(1)}, u32[]{:S(2)}, u32[]{:S(2)}) async-start(f32[2,256,128]{2,0,1:T(2,128)} %copy.114), calls=%async_computation.1 | async-start | bytes 524288 | tf_op jit(solution)/shard_map/all_to_all | solution.py:138
Sparse Core Ops, SparseCore 0:
  82.2 57.1 reduce-scatter.1
where the time goes:
time: 164 us; the launch traced here: 163 us
  waiting for transfers between devices  67.9 us (41%)
  blocking collectives  25.5 us (16%)
  local copies, waits for them, and re-layouts  23 us (14%)
  starting transfers between devices  21 us (13%)
  between operations  15 us (9%)
  other arithmetic  7.95 us (5%)
  matrix products  2.92 us (2%)
    reduce_scatter x1, waiting for transfers between devices, per_device(): lax.psum_scatter(projected, ('gx', 'gy'), scatter_dimension=1, tiled=True)  57 us
    all_gather x1, blocking collectives, per_device(): lax.all_gather(sample_rows, ('gx', 'gz'), axis=0, tiled=True)  16.7 us
    ppermute x3, starting transfers between devices, padded_2(): lax.ppermute(lax.slice_in_dim(block, block.shape[dim] - width, None, axis...  13.3 us
    all_to_all x1, waiting for transfers between devices, per_device(): lax.all_to_all(spectra, ('gx', 'gy'), split_axis=1, concat_axis=2, tiled=...  9.27 us
    unnamed x1, blocking collectives  8.8 us
    unnamed x22, local copies, waits for them, and re-layouts  7.35 us
    ppermute x3, starting transfers between devices, padded_2(): lax.ppermute(lax.slice_in_dim(block, 0, width, axis=dim), axis, backward)  3.86 us
    all_to_all x1, starting transfers between devices, per_device(): lax.all_to_all(spectra, ('gx', 'gy'), split_axis=1, concat_axis=2, tiled=...  3.74 us
  transfers between devices with their start and end apart: 8, of which 3 were waited for; matrix products, arithmetic and copies ran while one was open for 6% of the time, Pallas kernels for 0%

commit v1 on v0

v1 whole, which is shorter than its diff:
```python
import functools
import math

import jax
import jax.numpy as jnp
import numpy as np
from jax import lax
from jax.experimental import pallas as pl
from jax.experimental.pallas import tpu as pltpu
from jax.sharding import PartitionSpec as P

FREQS = 256
MESH = pl.DeviceIdType.MESH


def spectral_rows(count, freqs, steps):
    times = np.arange(steps, dtype=np.float64)
    levels = np.arange(count, dtype=np.float64) + 0.5
    phase = math.pi / (2.0 * freqs) * levels[:, None] * times[None, :]
    scale = 1.0 / math.sqrt(steps)
    return np.stack([np.cos(phase) * scale, -np.sin(phase) * scale]).astype(np.float32)


def kernel(
    n_gx, n_gy, n_gz, cap, rows,
    decay, gain, e_ref, h_ref, perm_ref, mask_ref, cells_ref, own_col, own_row, hist_ref,
    table_ref, poles_hbm, steer_hbm,
    e_out, h_out, far_out, poles_out_hbm,
    poles, poles_out, steer, edge_j, edge_k, got_i, got_j, got_k,
    low_j, low_k, from_i, from_j, from_k, compact, tile, part, got_1, got_2, got_3, full,
    local_sem, halo_send, halo_recv, tile_send, tile_recv,
    core_send, core_recv, mid_send, mid_recv, end_send, end_recv,
    back_z_send, back_z_recv, back_x_send, back_x_recv, back_c_send, back_c_recv,
):
    gx, gy, gz = lax.axis_index("gx"), lax.axis_index("gy"), lax.axis_index("gz")
    n_x = n_gx // 2
    core, mid = lax.rem(gx, 2), gx // 2
    span_x, span_y, span_z = e_ref.shape[1:]

    load_poles = pltpu.make_async_copy(poles_hbm, poles, local_sem.at[0])
    load_poles.start()
    load_steer = pltpu.make_async_copy(steer_hbm, steer, local_sem.at[1])
    load_steer.start()

    barrier = pltpu.get_barrier_semaphore()
    partners = 0
    for da in range(n_gx):
        for dz in range(n_gz):
            if da or dz:
                peer = (lax.rem(gx + da, n_gx), gy, lax.rem(gz + dz, n_gz))
                pl.semaphore_signal(barrier, inc=1, device_id=peer, device_id_type=MESH)
                partners += 1
    for dw in range(1, n_gy):
        peer = (gx, lax.rem(gy + dw, n_gy), gz)
        pl.semaphore_signal(barrier, inc=1, device_id=peer, device_id_type=MESH)
        partners += 1
    pl.semaphore_wait(barrier, partners)

    def remote(src, dst, send, recv, peer):
        return pltpu.make_async_remote_copy(
            src_ref=src, dst_ref=dst, send_sem=send, recv_sem=recv,
            device_id=peer, device_id_type=MESH,
        )

    flat = (span_x * span_y, span_z)
    cells = (span_x, span_y, span_z)

    def column(field, lane):
        return jnp.transpose(field.reshape(flat))[lane : lane + 1]

    def spread(row):
        return jnp.transpose(jnp.broadcast_to(row, (span_z, flat[0]))).reshape(cells)

    up_i = remote(e_ref.at[pl.ds(1, 2), 0], got_i, halo_send.at[0], halo_recv.at[0], (gx - 1, gy, gz))
    up_j = remote(edge_j, got_j, halo_send.at[1], halo_recv.at[1], (gx, gy - 1, gz))
    up_k = remote(edge_k, got_k, halo_send.at[2], halo_recv.at[2], (gx, gy, gz - 1))
    down_i = remote(
        h_out.at[pl.ds(1, 2), span_x - 1], from_i, halo_send.at[3], halo_recv.at[3], (gx + 1, gy, gz)
    )
    down_j = remote(low_j, from_j, halo_send.at[4], halo_recv.at[4], (gx, gy + 1, gz))
    down_k = remote(low_k, from_k, halo_send.at[5], halo_recv.at[5], (gx, gy, gz + 1))

    @pl.when(gz > 0)
    def _():
        edge_k[0:1] = column(e_ref[0], 0)
        edge_k[1:2] = column(e_ref[1], 0)
        edge_k[2:8] = jnp.zeros((6, flat[0]), jnp.float32)
        up_k.start()

    @pl.when(gx > 0)
    def _():
        up_i.start()

    @pl.when(gy > 0)
    def _():
        edge_j[0] = e_ref[0, :, 0, :]
        edge_j[1] = e_ref[2, :, 0, :]
        up_j.start()

    @pl.when(gx == n_gx - 1)
    def _():
        got_i[...] = jnp.zeros(got_i.shape, jnp.float32)

    @pl.when(gy == n_gy - 1)
    def _():
        got_j[...] = jnp.zeros(got_j.shape, jnp.float32)

    @pl.when(gz == n_gz - 1)
    def _():
        got_k[...] = jnp.zeros(got_k.shape, jnp.float32)

    @pl.when(gx == 0)
    def _():
        from_i[...] = jnp.zeros(from_i.shape, jnp.float32)

    @pl.when(gy == 0)
    def _():
        from_j[...] = jnp.zeros(from_j.shape, jnp.float32)

    @pl.when(gz == 0)
    def _():
        from_k[...] = jnp.zeros(from_k.shape, jnp.float32)

    count = own_col.shape[0]
    earlier = lax.broadcasted_iota(jnp.int32, (count, count), 0) < lax.broadcasted_iota(
        jnp.int32, (count, count), 1
    )
    same = jnp.where((own_col[...] == own_row[...]) & earlier, 1.0, 0.0)
    rank = jnp.sum(same, axis=0, keepdims=True).astype(jnp.int32)
    slot = own_row[...] * rows + rank
    place = (
        lax.broadcasted_iota(jnp.int32, (n_gx * rows, count), 0) == slot
    ).astype(jnp.float32).astype(jnp.bfloat16)

    at_j = lax.broadcasted_iota(jnp.int32, cells, 1)
    at_k = lax.broadcasted_iota(jnp.int32, cells, 2)

    def next_j(field, halo):
        return jnp.where(at_j == span_y - 1, halo[:, None, :], pltpu.roll(field, span_y - 1, 1))

    def next_k(field, halo):
        return jnp.where(at_k == span_z - 1, spread(halo), pltpu.roll(field, span_z - 1, 2))

    def prev_j(field, halo):
        return jnp.where(at_j == 0, halo[:, None, :], pltpu.roll(field, 1, 1))

    def prev_k(field, halo):
        return jnp.where(at_k == 0, spread(halo), pltpu.roll(field, 1, 2))

    @pl.when(gx < n_gx - 1)
    def _():
        up_i.wait_recv()

    @pl.when(gy < n_gy - 1)
    def _():
        up_j.wait_recv()

    @pl.when(gz < n_gz - 1)
    def _():
        up_k.wait_recv()

    ex, ey, ez = e_ref[0], e_ref[1], e_ref[2]
    ey_i = jnp.concatenate([ey[1:], got_i[0][None]], axis=0)
    ez_i = jnp.concatenate([ez[1:], got_i[1][None]], axis=0)
    mag_x = h_ref[0] - 0.5 * (next_j(ez, got_j[1]) - ez - (next_k(ey, got_k[1:2]) - ey))
    h_out[0] = mag_x
    mag_y = h_ref[1] - 0.5 * (next_k(ex, got_k[0:1]) - ex - (ez_i - ez))
    h_out[1] = mag_y
    mag_z = h_ref[2] - 0.5 * (ey_i - ey - (next_j(ex, got_j[0]) - ex))
    h_out[2] = mag_z

    @pl.when(gx < n_gx - 1)
    def _():
        down_i.start()

    @pl.when(gz < n_gz - 1)
    def _():
        low_k[0:1] = column(h_out[0], span_z - 1)
        low_k[1:2] = column(h_out[1], span_z - 1)
        low_k[2:8] = jnp.zeros((6, flat[0]), jnp.float32)
        down_k.start()

    @pl.when(gy < n_gy - 1)
    def _():
        low_j[0] = h_out[0, :, span_y - 1, :]
        low_j[1] = h_out[2, :, span_y - 1, :]
        down_j.start()

    load_poles.wait()

    @pl.when(gx > 0)
    def _():
        down_i.wait_recv()

    @pl.when(gy > 0)
    def _():
        down_j.wait_recv()

    @pl.when(gz > 0)
    def _():
        down_k.wait_recv()

    mag_x, mag_y, mag_z = h_out[0], h_out[1], h_out[2]
    mag_y_i = jnp.concatenate([from_i[0][None], mag_y[:-1]], axis=0)
    mag_z_i = jnp.concatenate([from_i[1][None], mag_z[:-1]], axis=0)
    drives = (
        mag_z - prev_j(mag_z, from_j[1]) - (mag_y - prev_k(mag_y, from_k[1:2])),
        mag_x - prev_k(mag_x, from_k[0:1]) - (mag_z - mag_z_i),
        mag_y - mag_y_i - (mag_x - prev_j(mag_x, from_j[0])),
    )
    wall = mask_ref[...] == 1
    half_eps = 0.5 / perm_ref[...]
    for comp in range(3):
        drive = drives[comp]
        total = None
        for pole in range(poles.shape[0]):
            state = decay[pole] * poles[pole, comp] + gain[pole] * drive
            poles_out[pole, comp] = state
            total = state if total is None else total + state
        e_out[comp] = jnp.where(wall, total, e_ref[comp] + half_eps * drive)
    store_poles = pltpu.make_async_copy(poles_out, poles_out_hbm, local_sem.at[2])
    store_poles.start()

    cell = cells_ref[...]
    row_hot = (
        lax.broadcasted_iota(jnp.int32, (count, flat[0]), 1) == cell // span_z
    ).astype(jnp.float32).astype(jnp.bfloat16)
    lane_hot = lax.broadcasted_iota(jnp.int32, (count, span_z), 1) == lax.rem(cell, span_z)
    steps = hist_ref.shape[1] // 4
    lane = lax.broadcasted_iota(jnp.int32, hist_ref.shape, 1)
    samples = hist_ref[...].astype(jnp.float32)
    for comp, field in enumerate((e_out[0], e_out[1], h_out[0], h_out[1])):
        found = jnp.dot(
            row_hot, field.reshape(flat).astype(jnp.bfloat16), preferred_element_type=jnp.float32
        )
        fresh = jnp.sum(jnp.where(lane_hot, found, 0.0), axis=1, keepdims=True)
        samples = jnp.where(lane == comp * steps + steps - 1, fresh, samples)
    packed = jnp.dot(
        place, samples.astype(jnp.bfloat16), preferred_element_type=jnp.float32
    ).astype(jnp.bfloat16)
    compact[...] = packed.reshape(compact.shape)
    me = gz * n_gx + gx
    tile_copies = []
    for da in range(n_gx):
        for dz in range(n_gz):
            to_x, to_z = lax.rem(gx + da, n_gx), lax.rem(gz + dz, n_gz)
            if da or dz:
                index = da * n_gz + dz
                copy = remote(
                    compact.at[to_x], tile.at[me], tile_send.at[index], tile_recv.at[index],
                    (to_x, gy, to_z),
                )
                copy.start()
                tile_copies.append(copy)
    tile[me] = compact[gx]
    load_steer.wait()
    for copy in tile_copies:
        copy.wait_recv()

    sources = n_gx * n_gz
    slots = tile[...].reshape(sources * rows, 4 * steps)
    if rows != cap:
        place_row = lax.broadcasted_iota(jnp.int32, (sources * cap, sources * rows), 0)
        place_col = lax.broadcasted_iota(jnp.int32, (sources * cap, sources * rows), 1)
        keep = (place_col == place_row // cap * rows + lax.rem(place_row, cap)).astype(jnp.float32)
        slots = jnp.dot(
            keep.astype(jnp.bfloat16), slots, preferred_element_type=jnp.float32
        ).astype(jnp.bfloat16)
    turned = jnp.transpose(slots.astype(jnp.float32)).astype(jnp.bfloat16)
    currents = jnp.concatenate(
        [turned[comp * steps : (comp + 1) * steps] for comp in range(4)], axis=1
    )
    depth = 4 * slots.shape[0]

    chunks = part.shape[0]
    half = chunks // 2
    piece = half // n_x
    own = piece // n_gy
    t_blocks = steps // 8
    width = piece // t_blocks * 128

    def fill(start):
        offset = pl.multiple_of(start // t_blocks * 128, 128)
        weights = steer[:, :, pl.ds(offset, width)].reshape(depth, width)
        out = jnp.dot(currents, weights, preferred_element_type=jnp.float32)
        for block in range(width // 128):
            part[pl.ds(start + block * t_blocks, t_blocks)] = out[
                :, block * 128 : (block + 1) * 128
            ].reshape(t_blocks, 8, 128)

    order_x = list(range(1, n_x)) + [0]
    order_z = list(range(1, n_gy)) + [0]
    sends = []

    def begin(copy):
        copy.start()
        sends.append(copy)
        return copy

    other = (mid * 2 + 1 - core, gy, gz)
    first = {}
    for dq in order_x:
        to = lax.rem(mid + dq, n_x)
        start = (1 - core) * half + to * piece
        fill(start)
        first[dq] = begin(
            remote(
                part.at[pl.ds(start, piece)], got_1.at[pl.ds(to * piece, piece)],
                core_send.at[dq], core_recv.at[dq], other,
            )
        )
    for dq in order_x:
        fill(core * half + lax.rem(mid + dq, n_x) * piece)
    second = {}
    for dq in order_x:
        to = lax.rem(mid + dq, n_x)
        start = core * half + to * piece
        first[dq].wait_recv()
        part[pl.ds(start, piece)] += got_1[pl.ds(to * piece, piece)]
        if dq:
            for dw in order_z:
                at = lax.rem(gy + dw, n_gy) * own
                second[dq, dw] = begin(
                    remote(
                        part.at[pl.ds(start + at, own)], got_2.at[dq - 1, pl.ds(at, own)],
                        mid_send.at[dq - 1, dw], mid_recv.at[dq - 1, dw], (to * 2 + core, gy, gz),
                    )
                )
    base = core * half + mid * piece
    third = {}
    for dw in order_z:
        to = lax.rem(gy + dw, n_gy)
        at = to * own
        for dq in range(1, n_x):
            second[dq, dw].wait_recv()
            part[pl.ds(base + at, own)] += got_2[dq - 1, pl.ds(at, own)]
        if dw:
            third[dw] = begin(
                remote(
                    part.at[pl.ds(base + at, own)], got_3.at[dw - 1],
                    end_send.at[dw - 1], end_recv.at[dw - 1], (gx, to, gz),
                )
            )
    mine = base + gy * own
    total = part[pl.ds(mine, own)]
    for dw in range(1, n_gy):
        third[dw].wait_recv()
        total = total + got_3[dw - 1]
    full[pl.ds(mine, own)] = total

    last = {}

    def to_core(start, dq, dw):
        block = full.at[pl.ds(start, own)]
        last[dq, dw] = begin(
            remote(block, block, back_c_send.at[dq, dw], back_c_recv.at[dq, dw], other)
        )

    wide = {}

    def to_mid(start, dw):
        block = full.at[pl.ds(start, own)]
        for dq in range(1, n_x):
            wide[dq, dw] = begin(
                remote(
                    block, block, back_x_send.at[dq - 1, dw], back_x_recv.at[dq - 1, dw],
                    (lax.rem(mid + dq, n_x) * 2 + core, gy, gz),
                )
            )

    long = {}
    for dw in range(1, n_gy):
        block = full.at[pl.ds(mine, own)]
        long[dw] = begin(
            remote(
                block, block, back_z_send.at[dw - 1], back_z_recv.at[dw - 1],
                (gx, lax.rem(gy + dw, n_gy), gz),
            )
        )
    to_mid(mine, 0)
    to_core(mine, 0, 0)
    for dw in range(1, n_gy):
        long[dw].wait_recv()
        start = base + lax.rem(gy + n_gy - dw, n_gy) * own
        to_mid(start, dw)
        to_core(start, 0, dw)
    for dw in range(n_gy):
        for dq in range(1, n_x):
            wide[dq, dw].wait_recv()
            start = (
                core * half
                + lax.rem(mid + n_x - dq, n_x) * piece
                + lax.rem(gy + n_gy - dw, n_gy) * own
            )
            to_core(start, dq, dw)
    for dw in range(n_gy):
        for dq in range(n_x):
            last[dq, dw].wait_recv()
    for block in range(chunks // t_blocks):
        values = full[pl.ds(block * t_blocks, t_blocks)].reshape(steps, 128)
        far_out[:, block * 128 : (block + 1) * 128] = jnp.dot(
            table_ref[...], values, precision=lax.Precision.HIGHEST,
            preferred_element_type=jnp.float32,
        )

    for copy in sends + tile_copies:
        copy.wait_send()
    store_poles.wait()

    @pl.when(gx > 0)
    def _():
        up_i.wait_send()

    @pl.when(gy > 0)
    def _():
        up_j.wait_send()

    @pl.when(gz > 0)
    def _():
        up_k.wait_send()

    @pl.when(gx < n_gx - 1)
    def _():
        down_i.wait_send()

    @pl.when(gy < n_gy - 1)
    def _():
        down_j.wait_send()

    @pl.when(gz < n_gz - 1)
    def _():
        down_k.wait_send()


def per_device(
    e_field, h_field, permittivity, wall_mask, poles, pole_decay, pole_gain,
    face_cells, owners, history, steering,
):
    n_gx, n_gy, n_gz = (lax.axis_size(axis) for axis in ("gx", "gy", "gz"))
    n_x = n_gx // 2
    count = face_cells.shape[0]
    steps = history.shape[0] + 1
    cap = steering.shape[1] // (n_gx * n_gz)
    rows = -(-cap // 16) * 16
    dirs = steering.shape[2]
    blocks = n_gx * n_gy
    mine = FREQS // blocks
    _, span_x, span_y, span_z = e_field.shape
    flat = span_x * span_y

    table = spectral_rows(FREQS, FREQS, steps)
    table = table.reshape(2, blocks, mine, steps).transpose(1, 0, 2, 3).reshape(blocks, 2 * mine, steps)
    rank = lax.axis_index("gx") * n_gy + lax.axis_index("gy")
    table = lax.dynamic_index_in_dim(jnp.asarray(table), rank, 0, keepdims=False)
    hist = jnp.pad(jnp.transpose(history, (2, 1, 0)), ((0, 0), (0, 0), (0, 1))).reshape(count, 4 * steps)

    chunks = steps // 8 * (dirs // 128)
    half = chunks // 2
    piece = half // n_x
    own = piece // n_gy
    f32, bf16 = jnp.float32, jnp.bfloat16
    dma = lambda *dims: pltpu.SemaphoreType.DMA(dims)
    vmem = pl.BlockSpec(memory_space=pltpu.VMEM)
    smem = pl.BlockSpec(memory_space=pltpu.SMEM)
    hbm = pl.BlockSpec(memory_space=pl.ANY)
    wide = max(n_x - 1, 1)
    e_next, h_next, far, poles_next = pl.pallas_call(
        functools.partial(kernel, n_gx, n_gy, n_gz, cap, rows),
        out_shape=(
            jax.ShapeDtypeStruct(e_field.shape, f32),
            jax.ShapeDtypeStruct(h_field.shape, f32),
            jax.ShapeDtypeStruct((2 * mine, dirs), f32),
            jax.ShapeDtypeStruct(poles.shape, f32),
        ),
        in_specs=[smem, smem] + [vmem] * 9 + [hbm, hbm],
        out_specs=(vmem, vmem, vmem, hbm),
        scratch_shapes=[
            pltpu.VMEM(poles.shape, f32),
            pltpu.VMEM(poles.shape, f32),
            pltpu.VMEM(steering.shape, bf16),
            pltpu.VMEM((2, span_x, span_z), f32),
            pltpu.VMEM((8, flat), f32),
            pltpu.VMEM((2, span_y, span_z), f32),
            pltpu.VMEM((2, span_x, span_z), f32),
            pltpu.VMEM((8, flat), f32),
            pltpu.VMEM((2, span_x, span_z), f32),
            pltpu.VMEM((8, flat), f32),
            pltpu.VMEM((2, span_y, span_z), f32),
            pltpu.VMEM((2, span_x, span_z), f32),
            pltpu.VMEM((8, flat), f32),
            pltpu.VMEM((n_gx, rows, 4 * steps), bf16),
            pltpu.VMEM((n_gx * n_gz, rows, 4 * steps), bf16),
            pltpu.VMEM((chunks, 8, 128), f32),
            pltpu.VMEM((half, 8, 128), f32),
            pltpu.VMEM((wide, piece, 8, 128), f32),
            pltpu.VMEM((n_gy - 1, own, 8, 128), f32),
            pltpu.VMEM((chunks, 8, 128), f32),
            dma(3), dma(6), dma(6), dma(n_gx * n_gz), dma(n_gx * n_gz),
            dma(n_x), dma(n_x), dma(wide, n_gy), dma(wide, n_gy), dma(n_gy - 1), dma(n_gy - 1),
            dma(n_gy - 1), dma(n_gy - 1), dma(wide, n_gy), dma(wide, n_gy), dma(n_x, n_gy), dma(n_x, n_gy),
        ],
        compiler_params=pltpu.CompilerParams(
            collective_id=0, has_side_effects=True, vmem_limit_bytes=32 * 1024 * 1024
        ),
    )(
        pole_decay, pole_gain, e_field, h_field, permittivity, wall_mask,
        face_cells[:, None], owners, owners.reshape(1, count), hist, table, poles, steering,
    )
    return (e_next, h_next, poles_next, far.reshape(2, mine, dirs))


def solution(mesh):
    return jax.shard_map(
        per_device,
        mesh=mesh,
        in_specs=(
            P(None, "gx", "gy", "gz"),
            P(None, "gx", "gy", "gz"),
            P("gx", "gy", "gz"),
            P("gx", "gy", "gz"),
            P(None, None, "gx", "gy", "gz"),
            P(),
            P(),
            P(("gx", "gy", "gz")),
            P(("gx", "gy", "gz"), None),
            P(None, None, ("gx", "gy", "gz")),
            P(None, ("gx", "gy"), "gz"),
        ),
        out_specs=(
            P(None, "gx", "gy", "gz"),
            P(None, "gx", "gy", "gz"),
            P(None, None, "gx", "gy", "gz"),
            P(None, ("gx", "gy"), "gz"),
        ),
        check_vma=False,
    )
```

time: 164 us -> 51.6 us (0.31)
  waiting for transfers between devices: 67.9 us -> 0 us
  Pallas kernels: 0 us -> 35.2 us
  blocking collectives: 25.5 us -> 0 us
  starting transfers between devices: 21 us -> 0 us
  between operations: 15 us -> 0.67 us
  local copies, waits for them, and re-layouts: 23 us -> 14.8 us
  other arithmetic: 7.95 us -> 0 us
  matrix products: 2.92 us -> 0 us
    reduce_scatter x1 -> x0, waiting for transfers between devices: 57 us -> none  [per_device(): lax.psum_scatter(projected, ('gx', 'gy'), scatter_dimension=1, tiled=True)]
    pallas_call x0 -> x1, Pallas kernels: none -> 35.2 us  [per_device(): pl.pallas_call(functools.partial(kernel, n_gx, n_gy, n_gz, cap, rows), ou...]
    ppermute x6 -> x0, starting transfers between devices: 17.2 us -> none  [the longest x3 13.3 us: padded_2(): lax.ppermute(lax.slice_in_dim(block, block.shape[dim] - width, None, axis...]
    all_gather x1 -> x0, blocking collectives: 16.7 us -> none  [per_device(): lax.all_gather(sample_rows, ('gx', 'gz'), axis=0, tiled=True)]
    all_to_all x1 -> x0, waiting for transfers between devices: 9.27 us -> none  [per_device(): lax.all_to_all(spectra, ('gx', 'gy'), split_axis=1, concat_axis=2, tiled=...]
    unnamed x1 -> x0, blocking collectives: 8.8 us -> none
    unnamed x22 -> x24, local copies, waits for them, and re-layouts: 7.35 us -> 13.2 us
    all_to_all x1 -> x0, starting transfers between devices: 3.74 us -> none  [per_device(): lax.all_to_all(spectra, ('gx', 'gy'), split_axis=1, concat_axis=2, tiled=...]
  transfers between devices with their start and end apart: 8 -> 0, of which waited for: 3 -> 0; matrix products, arithmetic and copies ran while one was open for 6% -> 0% of each run, Pallas kernels for 0% -> 0%
where the time goes in v1:
time: 51.6 us; the launch traced here: 50.7 us
  Pallas kernels  35.2 us (68%)
  local copies, waits for them, and re-layouts  14.8 us (29%)
  between operations  0.67 us (1%)
    pallas_call x1, Pallas kernels, per_device(): pl.pallas_call(functools.partial(kernel, n_gx, n_gy, n_gz, cap, rows), ou...  35.2 us
    unnamed x24, local copies, waits for them, and re-layouts  13.2 us

profile of v1, /device:TPU:0, one launch (start us, length us, event | category | flops | bytes accessed | tf_op | source)
XLA Modules:
  0.0 50.7 jit_solution(2725062166081017397)
XLA Ops:
  0.6 0.7 %dynamic-slice_bitcast_fusion.table_ref = f32[32,64]{1,0:T(8,128)S(1)} fusion(f32[16,32,64]{2,1,0:T(8,128)} %constant.22.clone, s32[]{:T(128)S(6)} %select_n.4), kind=kLoop, calls=%fused_computation | loop fusion | bytes 16388 | tf_op jit(solution)/shard_map/jit(dynamic_index_in_dim)/squeeze | solution.py:454
  1.4 0.7 %copy.17.cells_ref = s32[32,1]{1,0:T(8,128)S(1)} copy(s32[32,1]{0,1:T(1,128)} %bitcast.9) | data formatting | bytes 256 | tf_op jit(solution)/shard_map/broadcast_in_dim | solution.py:507
  2.1 0.7 %copy.18.own_col = s32[32,1]{1,0:T(8,128)S(1)} copy(s32[32,1]{0,1:T(1,128)} %param.20) | data formatting | bytes 256 | tf_op args[8]
  2.8 0.8 %copy.19 = bf16[32,4,63]{2,1,0:T(4,128)(2,1)S(1)} copy(bf16[32,4,63]{2,0,1:T(8,128)(2,1)} %bitcast.8) | data formatting | bytes 32256
  3.6 0.1 reshape.18.hist_ref
  3.7 0.0 copy-start
  3.7 1.6 %copy-done = bf16[4,128,2048]{2,1,0:T(8,128)(2,1)S(1)} copy-done((bf16[4,128,2048]{2,1,0:T(8,128)(2,1)S(1)}, bf16[4,128,2048]{2,1,0:T(8,128)(2,1)}, u32[]{:S(2)}) %copy-start) | copy-done | bytes 2097176
  5.3 0.0 copy-start.1
  5.3 1.4 %copy-done.1 = f32[8,3,8,16,128]{4,3,2,1,0:T(8,128)S(1)} copy-done((f32[8,3,8,16,128]{4,3,2,1,0:T(8,128)S(1)}, f32[8,3,8,16,128]{4,3,2,1,0:T(8,128)}, u32[]{:S(2)}) %copy-start.1) | copy-done | bytes 1572888
  6.7 0.0 copy-start.2
  6.7 0.9 %copy-done.2 = f32[3,8,16,128]{3,2,1,0:T(8,128)S(1)} copy-done((f32[3,8,16,128]{3,2,1,0:T(8,128)S(1)}, f32[3,8,16,128]{3,2,1,0:T(8,128)}, u32[]{:S(2)}) %copy-start.2) | copy-done | bytes 196632
  7.7 0.0 copy-start.3
  7.7 0.9 %copy-done.3 = f32[3,8,16,128]{3,2,1,0:T(8,128)S(1)} copy-done((f32[3,8,16,128]{3,2,1,0:T(8,128)S(1)}, f32[3,8,16,128]{3,2,1,0:T(8,128)}, u32[]{:S(2)}) %copy-start.3) | copy-done | bytes 196632
  8.6 0.0 copy-start.4
  8.6 0.8 %copy-done.4 = f32[8,16,128]{2,1,0:T(8,128)S(1)} copy-done((f32[8,16,128]{2,1,0:T(8,128)S(1)}, f32[8,16,128]{2,1,0:T(8,128)}, u32[]{:S(2)}) %copy-start.4) | copy-done | bytes 65560
  9.4 0.8 %copy-done.5 = s32[8,16,128]{2,1,0:T(8,128)S(1)} copy-done((s32[8,16,128]{2,1,0:T(8,128)S(1)}, s32[8,16,128]{2,1,0:T(8,128)}, u32[]{:S(2)}) %copy-start.5) | copy-done | bytes 65560
  10.3 0.7 %copy-done.6 = s32[32,1]{0,1:T(1,128)S(1)} copy-done((s32[32,1]{0,1:T(1,128)S(1)}, s32[32,1]{0,1:T(1,128)}, u32[]{:S(2)}) %copy-start.6) | copy-done | bytes 152
  10.9 0.7 %copy-done.7 = f32[8]{0:T(128)S(1)} copy-done((f32[8]{0:T(128)S(1)}, f32[8]{0:T(128)}, u32[]{:S(2)}) %copy-start.7) | copy-done | bytes 56
  11.6 0.7 %copy-done.8 = f32[8]{0:T(128)S(1)} copy-done((f32[8]{0:T(128)S(1)}, f32[8]{0:T(128)}, u32[]{:S(2)}) %copy-start.8) | copy-done | bytes 56
  12.2 35.2 %shard_map.147 = (f32[3,8,16,128]{3,2,1,0:T(8,128)S(1)}, f32[3,8,16,128]{3,2,1,0:T(8,128)S(1)}, f32[32,2048]{1,0:T(8,128)S(1)}, f32[8,3,8,16,128]{4,3,2,1,0:T(8,128)S(1)}) custom-call(f32[8]{0:T(128)S(1)} %copy-done.7, f32[8]{0:T(128)S(1)} %copy-done.8, f32[3,8,16,128]{3,2,1,0:T(8,128)S(1)} %copy-done.2, f32[3,8,16,128]{3,2,1,0:T(8,128)S(1)} %copy-done.3, ...), custom_call_target="tpu_custom_call" | custom-call | tf_op jit(solution)/shard_map/pallas_call | solution.py:467
  47.5 0.7 %copy.24 = f32[3,8,16,128]{3,2,1,0:T(8,128)} copy(f32[3,8,16,128]{3,2,1,0:T(8,128)S(1)} %get-tuple-element.16) | data formatting | bytes 393216
  48.2 0.7 %copy.25 = f32[3,8,16,128]{3,2,1,0:T(8,128)} copy(f32[3,8,16,128]{3,2,1,0:T(8,128)S(1)} %get-tuple-element.17) | data formatting | bytes 393216
  48.8 1.1 %copy.26 = f32[8,3,8,16,128]{4,3,2,1,0:T(8,128)} copy(f32[8,3,8,16,128]{4,3,2,1,0:T(8,128)S(1)} %get-tuple-element.18) | data formatting | bytes 3145728
  50.0 0.7 %copy.27 = f32[2,16,2048]{2,1,0:T(8,128)} copy(f32[2,16,2048]{2,1,0:T(8,128)S(1)} %bitcast.6) | data formatting | bytes 524288
  (5 shorter events, 0.0 us)
Async XLA Ops:
  3.7 1.6 %copy-start = (bf16[4,128,2048]{2,1,0:T(8,128)(2,1)S(1)}, bf16[4,128,2048]{2,1,0:T(8,128)(2,1)}, u32[]{:S(2)}) copy-start(bf16[4,128,2048]{2,1,0:T(8,128)(2,1)} %steer_hbm.1) | copy-start | bytes 6291460
  5.3 1.4 %copy-start.1 = (f32[8,3,8,16,128]{4,3,2,1,0:T(8,128)S(1)}, f32[8,3,8,16,128]{4,3,2,1,0:T(8,128)}, u32[]{:S(2)}) copy-start(f32[8,3,8,16,128]{4,3,2,1,0:T(8,128)} %poles_hbm.1) | copy-start | bytes 4718596
  6.7 0.9 %copy-start.2 = (f32[3,8,16,128]{3,2,1,0:T(8,128)S(1)}, f32[3,8,16,128]{3,2,1,0:T(8,128)}, u32[]{:S(2)}) copy-start(f32[3,8,16,128]{3,2,1,0:T(8,128)} %e_ref.1) | copy-start | bytes 589828
  7.7 0.9 %copy-start.3 = (f32[3,8,16,128]{3,2,1,0:T(8,128)S(1)}, f32[3,8,16,128]{3,2,1,0:T(8,128)}, u32[]{:S(2)}) copy-start(f32[3,8,16,128]{3,2,1,0:T(8,128)} %h_ref.1) | copy-start | bytes 589828
  8.6 0.8 %copy-start.4 = (f32[8,16,128]{2,1,0:T(8,128)S(1)}, f32[8,16,128]{2,1,0:T(8,128)}, u32[]{:S(2)}) copy-start(f32[8,16,128]{2,1,0:T(8,128)} %perm_ref.1) | copy-start | bytes 196612
  9.4 0.8 %copy-start.5 = (s32[8,16,128]{2,1,0:T(8,128)S(1)}, s32[8,16,128]{2,1,0:T(8,128)}, u32[]{:S(2)}) copy-start(s32[8,16,128]{2,1,0:T(8,128)} %mask_ref.1) | copy-start | bytes 196612
  10.3 0.7 %copy-start.6 = (s32[32,1]{0,1:T(1,128)S(1)}, s32[32,1]{0,1:T(1,128)}, u32[]{:S(2)}) copy-start(s32[32,1]{0,1:T(1,128)} %param.20) | copy-start | bytes 388
  10.9 0.7 %copy-start.7 = (f32[8]{0:T(128)S(1)}, f32[8]{0:T(128)}, u32[]{:S(2)}) copy-start(f32[8]{0:T(128)} %decay.1) | copy-start | bytes 100
  11.6 0.7 %copy-start.8 = (f32[8]{0:T(128)S(1)}, f32[8]{0:T(128)}, u32[]{:S(2)}) copy-start(f32[8]{0:T(128)} %gain.1) | copy-start | bytes 100

commit v2 on v1

--- a/solution.py
+++ b/solution.py
@@ -23,10 +23,11 @@
 
 def kernel(
     n_gx, n_gy, n_gz, cap, rows,
-    decay, gain, e_ref, h_ref, perm_ref, mask_ref, cells_ref, own_col, own_row, hist_ref,
-    table_ref, poles_hbm, steer_hbm,
-    e_out, h_out, far_out, poles_out_hbm,
-    poles, poles_out, steer, edge_j, edge_k, got_i, got_j, got_k,
+    decay_hbm, gain_hbm, e_hbm, h_hbm, perm_hbm, mask_hbm, cells_hbm, owners_hbm, hist_hbm,
+    table_hbm, poles_hbm, steer_hbm,
+    e_out, h_out, far_out, poles_out,
+    decay, gain, e_ref, h_ref, perm_ref, mask_ref, cells_ref, own_ref, hist_ref, table_ref,
+    poles, steer, edge_j, edge_k, got_i, got_j, got_k,
     low_j, low_k, from_i, from_j, from_k, compact, tile, part, got_1, got_2, got_3, full,
     local_sem, halo_send, halo_recv, tile_send, tile_recv,
     core_send, core_recv, mid_send, mid_recv, end_send, end_recv,
@@ -37,10 +38,18 @@
     core, mid = lax.rem(gx, 2), gx // 2
     span_x, span_y, span_z = e_ref.shape[1:]
 
-    load_poles = pltpu.make_async_copy(poles_hbm, poles, local_sem.at[0])
-    load_poles.start()
-    load_steer = pltpu.make_async_copy(steer_hbm, steer, local_sem.at[1])
-    load_steer.start()
+    block = gx * n_gy + gy
+    loads = [
+        pltpu.make_async_copy(source, target, local_sem.at[index])
+        for index, (source, target) in enumerate((
+            (e_hbm, e_ref), (h_hbm, h_ref), (owners_hbm, own_ref), (hist_hbm, hist_ref),
+            (cells_hbm, cells_ref), (steer_hbm, steer), (poles_hbm, poles), (perm_hbm, perm_ref),
+            (mask_hbm, mask_ref), (decay_hbm, decay), (gain_hbm, gain),
+            (table_hbm.at[block], table_ref),
+        ))
+    ]
+    for load in loads:
+        load.start()
 
     barrier = pltpu.get_barrier_semaphore()
     partners = 0
@@ -80,6 +89,8 @@
     down_j = remote(low_j, from_j, halo_send.at[4], halo_recv.at[4], (gx, gy + 1, gz))
     down_k = remote(low_k, from_k, halo_send.at[5], halo_recv.at[5], (gx, gy, gz + 1))
 
+    loads[0].wait()
+
     @pl.when(gz > 0)
     def _():
         edge_k[0:1] = column(e_ref[0], 0)
@@ -121,13 +132,20 @@
     def _():
         from_k[...] = jnp.zeros(from_k.shape, jnp.float32)
 
-    count = own_col.shape[0]
-    earlier = lax.broadcasted_iota(jnp.int32, (count, count), 0) < lax.broadcasted_iota(
-        jnp.int32, (count, count), 1
-    )
-    same = jnp.where((own_col[...] == own_row[...]) & earlier, 1.0, 0.0)
+    for load in loads[1:5]:
+        load.wait()
+    count = own_ref.shape[1]
+    sample = lax.broadcasted_iota(jnp.int32, (count, count), 0)
+    other_sample = lax.broadcasted_iota(jnp.int32, (count, count), 1)
+
+    def upright(row):
+        kept = jnp.where(sample == other_sample, row.astype(jnp.float32), 0.0)
+        return jnp.sum(kept, axis=1, keepdims=True).astype(jnp.int32)
+
+    own_row = own_ref[...]
+    same = jnp.where((upright(own_row) == own_row) & (sample < other_sample), 1.0, 0.0)
     rank = jnp.sum(same, axis=0, keepdims=True).astype(jnp.int32)
-    slot = own_row[...] * rows + rank
+    slot = own_row * rows + rank
     place = (
         lax.broadcasted_iota(jnp.int32, (n_gx * rows, count), 0) == slot
     ).astype(jnp.float32).astype(jnp.bfloat16)
@@ -186,7 +204,8 @@
         low_j[1] = h_out[2, :, span_y - 1, :]
         down_j.start()
 
-    load_poles.wait()
+    for load in loads[6:11]:
+        load.wait()
 
     @pl.when(gx > 0)
     def _():
@@ -218,17 +237,21 @@
             poles_out[pole, comp] = state
             total = state if total is None else total + state
         e_out[comp] = jnp.where(wall, total, e_ref[comp] + half_eps * drive)
-    store_poles = pltpu.make_async_copy(poles_out, poles_out_hbm, local_sem.at[2])
-    store_poles.start()
-
-    cell = cells_ref[...]
+
+    cell = upright(cells_ref[...])
     row_hot = (
         lax.broadcasted_iota(jnp.int32, (count, flat[0]), 1) == cell // span_z
     ).astype(jnp.float32).astype(jnp.bfloat16)
     lane_hot = lax.broadcasted_iota(jnp.int32, (count, span_z), 1) == lax.rem(cell, span_z)
-    steps = hist_ref.shape[1] // 4
-    lane = lax.broadcasted_iota(jnp.int32, hist_ref.shape, 1)
-    samples = hist_ref[...].astype(jnp.float32)
+    past = hist_ref.shape[2]
+    steps = past + 1
+    lane = lax.broadcasted_iota(jnp.int32, (count, 4 * steps), 1)
+    samples = jnp.zeros((count, 4 * steps), jnp.float32)
+    step_in = lax.broadcasted_iota(jnp.int32, (past, 4 * steps), 0)
+    step_out = lax.broadcasted_iota(jnp.int32, (past, 4 * steps), 1)
+    for comp in range(4):
+        spot = (step_out == step_in + comp * steps).astype(jnp.float32).astype(jnp.bfloat16)
+        samples += jnp.dot(hist_ref[comp], spot, preferred_element_type=jnp.float32)
     for comp, field in enumerate((e_out[0], e_out[1], h_out[0], h_out[1])):
         found = jnp.dot(
             row_hot, field.reshape(flat).astype(jnp.bfloat16), preferred_element_type=jnp.float32
@@ -253,7 +276,8 @@
                 copy.start()
                 tile_copies.append(copy)
     tile[me] = compact[gx]
-    load_steer.wait()
+    loads[5].wait()
+    loads[11].wait()
     for copy in tile_copies:
         copy.wait_recv()
 
@@ -405,7 +429,6 @@
 
     for copy in sends + tile_copies:
         copy.wait_send()
-    store_poles.wait()
 
     @pl.when(gx > 0)
     def _():
@@ -430,6 +453,16 @@
     @pl.when(gz < n_gz - 1)
     def _():
         down_k.wait_send()
+
+
+def hand_out(*refs):
+    copies = [
+        pltpu.make_async_copy(refs[index], refs[4 + index], refs[8].at[index]) for index in range(4)
+    ]
+    for copy in copies:
+        copy.start()
+    for copy in copies:
+        copy.wait()
 
 
 def per_device(
@@ -450,9 +483,7 @@
 
     table = spectral_rows(FREQS, FREQS, steps)
     table = table.reshape(2, blocks, mine, steps).transpose(1, 0, 2, 3).reshape(blocks, 2 * mine, steps)
-    rank = lax.axis_index("gx") * n_gy + lax.axis_index("gy")
-    table = lax.dynamic_index_in_dim(jnp.asarray(table), rank, 0, keepdims=False)
-    hist = jnp.pad(jnp.transpose(history, (2, 1, 0)), ((0, 0), (0, 0), (0, 1))).reshape(count, 4 * steps)
+    hist = jnp.transpose(history, (1, 2, 0))
 
     chunks = steps // 8 * (dirs // 128)
     half = chunks // 2
@@ -461,8 +492,7 @@
     f32, bf16 = jnp.float32, jnp.bfloat16
     dma = lambda *dims: pltpu.SemaphoreType.DMA(dims)
     vmem = pl.BlockSpec(memory_space=pltpu.VMEM)
-    smem = pl.BlockSpec(memory_space=pltpu.SMEM)
-    hbm = pl.BlockSpec(memory_space=pl.ANY)
+    hbm = pl.BlockSpec(memory_space=pltpu.HBM)
     wide = max(n_x - 1, 1)
     e_next, h_next, far, poles_next = pl.pallas_call(
         functools.partial(kernel, n_gx, n_gy, n_gz, cap, rows),
@@ -472,10 +502,19 @@
             jax.ShapeDtypeStruct((2 * mine, dirs), f32),
             jax.ShapeDtypeStruct(poles.shape, f32),
         ),
-        in_specs=[smem, smem] + [vmem] * 9 + [hbm, hbm],
-        out_specs=(vmem, vmem, vmem, hbm),
+        in_specs=[hbm] * 12,
+        out_specs=(vmem, vmem, vmem, vmem),
         scratch_shapes=[
-            pltpu.VMEM(poles.shape, f32),
+            pltpu.SMEM(pole_decay.shape, f32),
+            pltpu.SMEM(pole_gain.shape, f32),
+            pltpu.VMEM(e_field.shape, f32),
+            pltpu.VMEM(h_field.shape, f32),
+            pltpu.VMEM(permittivity.shape, f32),
+            pltpu.VMEM(wall_mask.shape, jnp.int32),
+            pltpu.VMEM((1, count), jnp.int32),
+            pltpu.VMEM((1, count), jnp.int32),
+            pltpu.VMEM(hist.shape, bf16),
+            pltpu.VMEM(table.shape[1:], f32),
             pltpu.VMEM(poles.shape, f32),
             pltpu.VMEM(steering.shape, bf16),
             pltpu.VMEM((2, span_x, span_z), f32),
@@ -495,7 +534,7 @@
             pltpu.VMEM((wide, piece, 8, 128), f32),
             pltpu.VMEM((n_gy - 1, own, 8, 128), f32),
             pltpu.VMEM((chunks, 8, 128), f32),
-            dma(3), dma(6), dma(6), dma(n_gx * n_gz), dma(n_gx * n_gz),
+            dma(12), dma(6), dma(6), dma(n_gx * n_gz), dma(n_gx * n_gz),
             dma(n_x), dma(n_x), dma(wide, n_gy), dma(wide, n_gy), dma(n_gy - 1), dma(n_gy - 1),
             dma(n_gy - 1), dma(n_gy - 1), dma(wide, n_gy), dma(wide, n_gy), dma(n_x, n_gy), dma(n_x, n_gy),
         ],
@@ -503,9 +542,22 @@
             collective_id=0, has_side_effects=True, vmem_limit_bytes=32 * 1024 * 1024
         ),
     )(
-        pole_decay, pole_gain, e_field, h_field, permittivity, wall_mask,
-        face_cells[:, None], owners, owners.reshape(1, count), hist, table, poles, steering,
+        *(
+            pltpu.with_memory_space_constraint(operand, pltpu.HBM)
+            for operand in (
+                pole_decay, pole_gain, e_field, h_field, permittivity, wall_mask, face_cells.reshape(1, count),
+                owners.reshape(1, count), hist, jnp.asarray(table), poles, steering,
+            )
+        )
     )
+    results = (e_next, h_next, poles_next, far)
+    e_next, h_next, poles_next, far = pl.pallas_call(
+        hand_out,
+        out_shape=tuple(jax.ShapeDtypeStruct(result.shape, f32) for result in results),
+        in_specs=[pl.BlockSpec(memory_space=pl.ANY)] * 4,
+        out_specs=(hbm,) * 4,
+        scratch_shapes=[dma(4)],
+    )(*results)
     return (e_next, h_next, poles_next, far.reshape(2, mine, dirs))
 
 

time: 51.6 us -> 108 us (2.09)
  Pallas kernels: 35.2 us -> 103 us
  local copies, waits for them, and re-layouts: 14.8 us -> 3.21 us
    pallas_call x0 -> x1, Pallas kernels: none -> 68.6 us  [per_device(): pl.pallas_call(hand_out, out_shape=tuple((jax.ShapeDtypeStruct(result.sha...]
    unnamed x24 -> x8, local copies, waits for them, and re-layouts: 13.2 us -> 3.21 us
where the time goes in v2:
time: 108 us; the launch traced here: 107 us
  Pallas kernels  103 us (95%)
  local copies, waits for them, and re-layouts  3.21 us (3%)
    pallas_call x1, Pallas kernels, per_device(): pl.pallas_call(hand_out, out_shape=tuple((jax.ShapeDtypeStruct(result.sha...  68.6 us
    pallas_call x1, Pallas kernels, per_device(): pl.pallas_call(functools.partial(kernel, n_gx, n_gy, n_gz, cap, rows), ou...  34.4 us
    unnamed x8, local copies, waits for them, and re-layouts  3.21 us

profile of v2, /device:TPU:0, one launch (start us, length us, event | category | flops | bytes accessed | tf_op | source)
XLA Modules:
  0.0 106.9 jit_solution(9519263142890639077)
XLA Ops:
  0.6 34.4 %shard_map.147 = (f32[3,8,16,128]{3,2,1,0:T(8,128)S(1)}, f32[3,8,16,128]{3,2,1,0:T(8,128)S(1)}, f32[32,2048]{1,0:T(8,128)S(1)}, f32[8,3,8,16,128]{4,3,2,1,0:T(8,128)S(1)}) custom-call(f32[8]{0:T(128)} %decay_hbm.1, f32[8]{0:T(128)} %gain_hbm.1, f32[3,8,16,128]{3,2,1,0:T(8,128)} %e_hbm.1, f32[3,8,16,128]{3,2,1,0:T(8,128)} %h_hbm.1, f32[8,16,128]{2,1,0:T(8,128)} %perm_hbm.1, ...), custom_call_target="tpu_custom_call" | custom-call | tf_op jit(solution)/shard_map/pallas_call | solution.py:497
  35.1 0.0 copy-start
  35.1 1.1 %copy-done = f32[8,3,8,16,128]{4,3,2,1,0:T(8,128)} copy-done((f32[8,3,8,16,128]{4,3,2,1,0:T(8,128)}, f32[8,3,8,16,128]{4,3,2,1,0:T(8,128)S(1)}, u32[]{:S(2)}) %copy-start) | copy-done | bytes 1572888
  36.2 0.0 copy-start.1
  36.2 0.7 copy-done.1
  36.9 0.0 copy-start.2
  36.9 0.7 copy-done.2
  37.6 0.0 copy-start.3
  37.6 0.7 copy-done.3
  38.3 68.6 %shard_map.148 = (f32[3,8,16,128]{3,2,1,0:T(8,128)}, f32[3,8,16,128]{3,2,1,0:T(8,128)}, f32[8,3,8,16,128]{4,3,2,1,0:T(8,128)}, f32[32,2048]{1,0:T(8,128)}) custom-call(f32[3,8,16,128]{3,2,1,0:T(8,128)} %copy-done.2, f32[3,8,16,128]{3,2,1,0:T(8,128)} %copy-done.3, f32[8,3,8,16,128]{4,3,2,1,0:T(8,128)} %copy-done, f32[32,2048]{1,0:T(8,128)} %copy-done.1), custom_call_target="tpu_custom_call" | custom-call | tf_op jit(solution)/shard_map/pallas_call | solution.py:554
Async XLA Ops:
  35.1 1.2 %copy-start = (f32[8,3,8,16,128]{4,3,2,1,0:T(8,128)}, f32[8,3,8,16,128]{4,3,2,1,0:T(8,128)S(1)}, u32[]{:S(2)}) copy-start(f32[8,3,8,16,128]{4,3,2,1,0:T(8,128)S(1)} %get-tuple-element.14.refs_2_) | copy-start | bytes 4718596
  36.2 0.7 copy-start.1
  36.9 0.7 copy-start.2
  37.6 0.7 copy-start.3

commit v3 on v2

--- a/solution.py
+++ b/solution.py
@@ -28,15 +28,24 @@
     e_out, h_out, far_out, poles_out,
     decay, gain, e_ref, h_ref, perm_ref, mask_ref, cells_ref, own_ref, hist_ref, table_ref,
     poles, steer, edge_j, edge_k, got_i, got_j, got_k,
-    low_j, low_k, from_i, from_j, from_k, compact, tile, part, got_1, got_2, got_3, full,
+    low_j, low_k, from_i, from_j, from_k, compact, tile, part, got_1, got_2, got_3, full, new_out, new_in, new_row, got_row,
     local_sem, halo_send, halo_recv, tile_send, tile_recv,
     core_send, core_recv, mid_send, mid_recv, end_send, end_recv,
-    back_z_send, back_z_recv, back_x_send, back_x_recv, back_c_send, back_c_recv,
+    new_send, new_recv, row_send, row_recv, back_z_send, back_z_recv, back_x_send, back_x_recv, back_c_send, back_c_recv,
 ):
     gx, gy, gz = lax.axis_index("gx"), lax.axis_index("gy"), lax.axis_index("gz")
     n_x = n_gx // 2
     core, mid = lax.rem(gx, 2), gx // 2
     span_x, span_y, span_z = e_ref.shape[1:]
+    count, past = hist_ref.shape[1:]
+    steps = past + 1
+    chunks = part.shape[0]
+    half = chunks // 2
+    piece = half // n_x
+    own = piece // n_gy
+    t_blocks = steps // 8
+    width = piece // t_blocks * 128
+    early = own % t_blocks == 0 and rows == cap
 
     block = gx * n_gy + gy
     loads = [
@@ -59,11 +68,11 @@
                 peer = (lax.rem(gx + da, n_gx), gy, lax.rem(gz + dz, n_gz))
                 pl.semaphore_signal(barrier, inc=1, device_id=peer, device_id_type=MESH)
                 partners += 1
-    for dw in range(1, n_gy):
-        peer = (gx, lax.rem(gy + dw, n_gy), gz)
-        pl.semaphore_signal(barrier, inc=1, device_id=peer, device_id_type=MESH)
-        partners += 1
-    pl.semaphore_wait(barrier, partners)
+    for da in range(n_gx if early else 1):
+        for dw in range(1, n_gy):
+            peer = (lax.rem(gx + da, n_gx), lax.rem(gy + dw, n_gy), gz)
+            pl.semaphore_signal(barrier, inc=1, device_id=peer, device_id_type=MESH)
+            partners += 1
 
     def remote(src, dst, send, recv, peer):
         return pltpu.make_async_remote_copy(
@@ -90,51 +99,14 @@
     down_k = remote(low_k, from_k, halo_send.at[5], halo_recv.at[5], (gx, gy, gz + 1))
 
     loads[0].wait()
-
-    @pl.when(gz > 0)
-    def _():
-        edge_k[0:1] = column(e_ref[0], 0)
-        edge_k[1:2] = column(e_ref[1], 0)
-        edge_k[2:8] = jnp.zeros((6, flat[0]), jnp.float32)
-        up_k.start()
-
-    @pl.when(gx > 0)
-    def _():
-        up_i.start()
-
-    @pl.when(gy > 0)
-    def _():
-        edge_j[0] = e_ref[0, :, 0, :]
-        edge_j[1] = e_ref[2, :, 0, :]
-        up_j.start()
-
-    @pl.when(gx == n_gx - 1)
-    def _():
-        got_i[...] = jnp.zeros(got_i.shape, jnp.float32)
-
-    @pl.when(gy == n_gy - 1)
-    def _():
-        got_j[...] = jnp.zeros(got_j.shape, jnp.float32)
-
-    @pl.when(gz == n_gz - 1)
-    def _():
-        got_k[...] = jnp.zeros(got_k.shape, jnp.float32)
-
-    @pl.when(gx == 0)
-    def _():
-        from_i[...] = jnp.zeros(from_i.shape, jnp.float32)
-
-    @pl.when(gy == 0)
-    def _():
-        from_j[...] = jnp.zeros(from_j.shape, jnp.float32)
-
-    @pl.when(gz == 0)
-    def _():
-        from_k[...] = jnp.zeros(from_k.shape, jnp.float32)
+    edge_k[0:1] = column(e_ref[0], 0)
+    edge_k[1:2] = column(e_ref[1], 0)
+    edge_k[2:8] = jnp.zeros((6, flat[0]), jnp.float32)
+    edge_j[0] = e_ref[0, :, 0, :]
+    edge_j[1] = e_ref[2, :, 0, :]
 
     for load in loads[1:5]:
         load.wait()
-    count = own_ref.shape[1]
     sample = lax.broadcasted_iota(jnp.int32, (count, count), 0)
     other_sample = lax.broadcasted_iota(jnp.int32, (count, count), 1)
 
@@ -149,6 +121,79 @@
     place = (
         lax.broadcasted_iota(jnp.int32, (n_gx * rows, count), 0) == slot
     ).astype(jnp.float32).astype(jnp.bfloat16)
+
+    lane = lax.broadcasted_iota(jnp.int32, (count, 4 * steps), 1)
+    samples = jnp.zeros((count, 4 * steps), jnp.float32)
+    step_in = lax.broadcasted_iota(jnp.int32, (past, 4 * steps), 0)
+    step_out = lax.broadcasted_iota(jnp.int32, (past, 4 * steps), 1)
+    for comp in range(4):
+        spot = (step_out == step_in + comp * steps).astype(jnp.float32).astype(jnp.bfloat16)
+        samples += jnp.dot(hist_ref[comp], spot, preferred_element_type=jnp.float32)
+    me = gz * n_gx + gx
+
+    def send(values, source, target, send_sem, recv_sem):
+        packed = jnp.dot(
+            place, values.astype(jnp.bfloat16), preferred_element_type=jnp.float32
+        ).astype(jnp.bfloat16)
+        source[...] = packed.reshape(source.shape)
+        copies = []
+        for da in range(n_gx):
+            for dz in range(n_gz):
+                to_x, to_z = lax.rem(gx + da, n_gx), lax.rem(gz + dz, n_gz)
+                if da or dz:
+                    index = da * n_gz + dz
+                    copy = remote(
+                        source.at[to_x], target.at[me], send_sem.at[index], recv_sem.at[index],
+                        (to_x, gy, to_z),
+                    )
+                    copy.start()
+                    copies.append(copy)
+        target[me] = source[gx]
+        return copies
+
+    def send_tiles():
+        return send(samples, compact, tile, tile_send, tile_recv)
+
+    pl.semaphore_wait(barrier, partners)
+
+    @pl.when(gz > 0)
+    def _():
+        up_k.start()
+
+    @pl.when(gx > 0)
+    def _():
+        up_i.start()
+
+    @pl.when(gy > 0)
+    def _():
+        up_j.start()
+
+    if early:
+        tile_copies = send_tiles()
+
+    @pl.when(gx == n_gx - 1)
+    def _():
+        got_i[...] = jnp.zeros(got_i.shape, jnp.float32)
+
+    @pl.when(gy == n_gy - 1)
+    def _():
+        got_j[...] = jnp.zeros(got_j.shape, jnp.float32)
+
+    @pl.when(gz == n_gz - 1)
+    def _():
+        got_k[...] = jnp.zeros(got_k.shape, jnp.float32)
+
+    @pl.when(gx == 0)
+    def _():
+        from_i[...] = jnp.zeros(from_i.shape, jnp.float32)
+
+    @pl.when(gy == 0)
+    def _():
+        from_j[...] = jnp.zeros(from_j.shape, jnp.float32)
+
+    @pl.when(gz == 0)
+    def _():
+        from_k[...] = jnp.zeros(from_k.shape, jnp.float32)
 
     at_j = lax.broadcasted_iota(jnp.int32, cells, 1)
     at_k = lax.broadcasted_iota(jnp.int32, cells, 2)
@@ -203,6 +248,79 @@
         low_j[0] = h_out[0, :, span_y - 1, :]
         low_j[1] = h_out[2, :, span_y - 1, :]
         down_j.start()
+
+    order_x = list(range(1, n_x)) + [0]
+    order_z = list(range(1, n_gy)) + [0]
+    sends = []
+
+    def begin(copy):
+        copy.start()
+        sends.append(copy)
+        return copy
+
+    other = (mid * 2 + 1 - core, gy, gz)
+    second = {}
+
+    def first_half(copies):
+        loads[5].wait()
+        loads[11].wait()
+        for copy in copies:
+            copy.wait_recv()
+
+        sources = n_gx * n_gz
+        slots = tile[...].reshape(sources * rows, 4 * steps)
+        if rows != cap:
+            place_row = lax.broadcasted_iota(jnp.int32, (sources * cap, sources * rows), 0)
+            place_col = lax.broadcasted_iota(jnp.int32, (sources * cap, sources * rows), 1)
+            keep = (place_col == place_row // cap * rows + lax.rem(place_row, cap)).astype(jnp.float32)
+            slots = jnp.dot(
+                keep.astype(jnp.bfloat16), slots, preferred_element_type=jnp.float32
+            ).astype(jnp.bfloat16)
+        turned = jnp.transpose(slots.astype(jnp.float32)).astype(jnp.bfloat16)
+        currents = jnp.concatenate(
+            [turned[comp * steps : (comp + 1) * steps] for comp in range(4)], axis=1
+        )
+        depth = 4 * slots.shape[0]
+
+        def fill(start):
+            offset = pl.multiple_of(start // t_blocks * 128, 128)
+            weights = steer[:, :, pl.ds(offset, width)].reshape(depth, width)
+            out = jnp.dot(currents, weights, preferred_element_type=jnp.float32)
+            for block in range(width // 128):
+                part[pl.ds(start + block * t_blocks, t_blocks)] = out[
+                    :, block * 128 : (block + 1) * 128
+                ].reshape(t_blocks, 8, 128)
+
+        first = {}
+        for dq in order_x:
+            to = lax.rem(mid + dq, n_x)
+            start = (1 - core) * half + to * piece
+            fill(start)
+            first[dq] = begin(
+                remote(
+                    part.at[pl.ds(start, piece)], got_1.at[pl.ds(to * piece, piece)],
+                    core_send.at[dq], core_recv.at[dq], other,
+                )
+            )
+        for dq in order_x:
+            fill(core * half + lax.rem(mid + dq, n_x) * piece)
+        for dq in order_x:
+            to = lax.rem(mid + dq, n_x)
+            start = core * half + to * piece
+            first[dq].wait_recv()
+            part[pl.ds(start, piece)] += got_1[pl.ds(to * piece, piece)]
+            if dq:
+                for dw in order_z:
+                    at = lax.rem(gy + dw, n_gy) * own
+                    second[dq, dw] = begin(
+                        remote(
+                            part.at[pl.ds(start + at, own)], got_2.at[dq - 1, pl.ds(at, own)],
+                            mid_send.at[dq - 1, dw], mid_recv.at[dq - 1, dw], (to * 2 + core, gy, gz),
+                        )
+                    )
+
+    if early:
+        first_half(tile_copies)
 
     for load in loads[6:11]:
         load.wait()
@@ -243,113 +361,22 @@
         lax.broadcasted_iota(jnp.int32, (count, flat[0]), 1) == cell // span_z
     ).astype(jnp.float32).astype(jnp.bfloat16)
     lane_hot = lax.broadcasted_iota(jnp.int32, (count, span_z), 1) == lax.rem(cell, span_z)
-    past = hist_ref.shape[2]
-    steps = past + 1
-    lane = lax.broadcasted_iota(jnp.int32, (count, 4 * steps), 1)
-    samples = jnp.zeros((count, 4 * steps), jnp.float32)
-    step_in = lax.broadcasted_iota(jnp.int32, (past, 4 * steps), 0)
-    step_out = lax.broadcasted_iota(jnp.int32, (past, 4 * steps), 1)
-    for comp in range(4):
-        spot = (step_out == step_in + comp * steps).astype(jnp.float32).astype(jnp.bfloat16)
-        samples += jnp.dot(hist_ref[comp], spot, preferred_element_type=jnp.float32)
+    fresh_lane = lax.broadcasted_iota(jnp.int32, (count, 128), 1)
+    fresh_all = jnp.zeros((count, 128), jnp.float32)
     for comp, field in enumerate((e_out[0], e_out[1], h_out[0], h_out[1])):
         found = jnp.dot(
             row_hot, field.reshape(flat).astype(jnp.bfloat16), preferred_element_type=jnp.float32
         )
         fresh = jnp.sum(jnp.where(lane_hot, found, 0.0), axis=1, keepdims=True)
-        samples = jnp.where(lane == comp * steps + steps - 1, fresh, samples)
-    packed = jnp.dot(
-        place, samples.astype(jnp.bfloat16), preferred_element_type=jnp.float32
-    ).astype(jnp.bfloat16)
-    compact[...] = packed.reshape(compact.shape)
-    me = gz * n_gx + gx
-    tile_copies = []
-    for da in range(n_gx):
-        for dz in range(n_gz):
-            to_x, to_z = lax.rem(gx + da, n_gx), lax.rem(gz + dz, n_gz)
-            if da or dz:
-                index = da * n_gz + dz
-                copy = remote(
-                    compact.at[to_x], tile.at[me], tile_send.at[index], tile_recv.at[index],
-                    (to_x, gy, to_z),
-                )
-                copy.start()
-                tile_copies.append(copy)
-    tile[me] = compact[gx]
-    loads[5].wait()
-    loads[11].wait()
-    for copy in tile_copies:
-        copy.wait_recv()
-
-    sources = n_gx * n_gz
-    slots = tile[...].reshape(sources * rows, 4 * steps)
-    if rows != cap:
-        place_row = lax.broadcasted_iota(jnp.int32, (sources * cap, sources * rows), 0)
-        place_col = lax.broadcasted_iota(jnp.int32, (sources * cap, sources * rows), 1)
-        keep = (place_col == place_row // cap * rows + lax.rem(place_row, cap)).astype(jnp.float32)
-        slots = jnp.dot(
-            keep.astype(jnp.bfloat16), slots, preferred_element_type=jnp.float32
-        ).astype(jnp.bfloat16)
-    turned = jnp.transpose(slots.astype(jnp.float32)).astype(jnp.bfloat16)
-    currents = jnp.concatenate(
-        [turned[comp * steps : (comp + 1) * steps] for comp in range(4)], axis=1
-    )
-    depth = 4 * slots.shape[0]
-
-    chunks = part.shape[0]
-    half = chunks // 2
-    piece = half // n_x
-    own = piece // n_gy
-    t_blocks = steps // 8
-    width = piece // t_blocks * 128
-
-    def fill(start):
-        offset = pl.multiple_of(start // t_blocks * 128, 128)
-        weights = steer[:, :, pl.ds(offset, width)].reshape(depth, width)
-        out = jnp.dot(currents, weights, preferred_element_type=jnp.float32)
-        for block in range(width // 128):
-            part[pl.ds(start + block * t_blocks, t_blocks)] = out[
-                :, block * 128 : (block + 1) * 128
-            ].reshape(t_blocks, 8, 128)
-
-    order_x = list(range(1, n_x)) + [0]
-    order_z = list(range(1, n_gy)) + [0]
-    sends = []
-
-    def begin(copy):
-        copy.start()
-        sends.append(copy)
-        return copy
-
-    other = (mid * 2 + 1 - core, gy, gz)
-    first = {}
-    for dq in order_x:
-        to = lax.rem(mid + dq, n_x)
-        start = (1 - core) * half + to * piece
-        fill(start)
-        first[dq] = begin(
-            remote(
-                part.at[pl.ds(start, piece)], got_1.at[pl.ds(to * piece, piece)],
-                core_send.at[dq], core_recv.at[dq], other,
-            )
-        )
-    for dq in order_x:
-        fill(core * half + lax.rem(mid + dq, n_x) * piece)
-    second = {}
-    for dq in order_x:
-        to = lax.rem(mid + dq, n_x)
-        start = core * half + to * piece
-        first[dq].wait_recv()
-        part[pl.ds(start, piece)] += got_1[pl.ds(to * piece, piece)]
-        if dq:
-            for dw in order_z:
-                at = lax.rem(gy + dw, n_gy) * own
-                second[dq, dw] = begin(
-                    remote(
-                        part.at[pl.ds(start + at, own)], got_2.at[dq - 1, pl.ds(at, own)],
-                        mid_send.at[dq - 1, dw], mid_recv.at[dq - 1, dw], (to * 2 + core, gy, gz),
-                    )
-                )
+        if early:
+            fresh_all = jnp.where(fresh_lane == comp, fresh, fresh_all)
+        else:
+            samples = jnp.where(lane == comp * steps + steps - 1, fresh, samples)
+    if early:
+        new_copies = send(fresh_all, new_out, new_in, new_send, new_recv)
+    else:
+        tile_copies = send_tiles()
+        first_half(tile_copies)
     base = core * half + mid * piece
     third = {}
     for dw in order_z:
@@ -366,11 +393,62 @@
                 )
             )
     mine = base + gy * own
+    rows_out = {}
+    if early:
+        for copy in new_copies:
+            copy.wait_recv()
+        turned = jnp.transpose(new_in[...].reshape(n_gx * n_gz * rows, 128).astype(jnp.float32))
+        line = jnp.concatenate([turned[comp : comp + 1] for comp in range(4)], axis=1)
+        line = jnp.broadcast_to(line, (16, line.shape[1])).astype(jnp.bfloat16)
+        for start in range(0, new_row.shape[0], 4):
+            weights = steer[:, :, start * 128 : (start + 4) * 128].reshape(line.shape[1], 512)
+            out = jnp.dot(line, weights, preferred_element_type=jnp.float32)
+            for index in range(4):
+                new_row[start + index] = out[0:1, index * 128 : (index + 1) * 128]
+        count_d = own // t_blocks
+        for da in range(n_gx):
+            for dw in range(n_gy):
+                if da or dw:
+                    to_x, to_y = lax.rem(gx + da, n_gx), lax.rem(gy + dw, n_gy)
+                    begin_d = (
+                        lax.rem(to_x, 2) * half + to_x // 2 * piece + to_y * own
+                    ) // t_blocks
+                    index = da * n_gy + dw
+                    rows_out[index] = begin(
+                        remote(
+                            new_row.at[pl.ds(begin_d, count_d)], got_row.at[index],
+                            row_send.at[index], row_recv.at[index], (to_x, to_y, gz),
+                        )
+                    )
     total = part[pl.ds(mine, own)]
     for dw in range(1, n_gy):
         third[dw].wait_recv()
         total = total + got_3[dw - 1]
     full[pl.ds(mine, own)] = total
+    if early:
+        added = new_row[pl.ds(mine // t_blocks, count_d)]
+        for index in rows_out:
+            rows_out[index].wait_recv()
+            added = added + got_row[index]
+        for index in range(count_d):
+            full[mine + (index + 1) * t_blocks - 1, 7:8, :] += added[index]
+
+    def transform(start, many):
+        for index in range(many // t_blocks):
+            at = start // t_blocks + index
+            values = full[pl.ds(at * t_blocks, t_blocks)].reshape(steps, 128)
+            if not isinstance(at, int):
+                at = pl.multiple_of(at * 128, 128)
+            else:
+                at = at * 128
+            far_out[:, pl.ds(at, 128)] = jnp.dot(
+                table_ref[...], values, precision=lax.Precision.HIGHEST,
+                preferred_element_type=jnp.float32,
+            )
+
+    def arrived(start):
+        if early:
+            transform(start, own)
 
     last = {}
 
@@ -403,11 +481,13 @@
         )
     to_mid(mine, 0)
     to_core(mine, 0, 0)
+    arrived(mine)
     for dw in range(1, n_gy):
         long[dw].wait_recv()
         start = base + lax.rem(gy + n_gy - dw, n_gy) * own
         to_mid(start, dw)
         to_core(start, 0, dw)
+        arrived(start)
     for dw in range(n_gy):
         for dq in range(1, n_x):
             wide[dq, dw].wait_recv()
@@ -417,17 +497,19 @@
                 + lax.rem(gy + n_gy - dw, n_gy) * own
             )
             to_core(start, dq, dw)
+            arrived(start)
     for dw in range(n_gy):
         for dq in range(n_x):
             last[dq, dw].wait_recv()
-    for block in range(chunks // t_blocks):
-        values = full[pl.ds(block * t_blocks, t_blocks)].reshape(steps, 128)
-        far_out[:, block * 128 : (block + 1) * 128] = jnp.dot(
-            table_ref[...], values, precision=lax.Precision.HIGHEST,
-            preferred_element_type=jnp.float32,
-        )
-
-    for copy in sends + tile_copies:
+            arrived(
+                (1 - core) * half
+                + lax.rem(mid + n_x - dq, n_x) * piece
+                + lax.rem(gy + n_gy - dw, n_gy) * own
+            )
+    if not early:
+        transform(0, chunks)
+
+    for copy in sends + tile_copies + (new_copies if early else []):
         copy.wait_send()
 
     @pl.when(gx > 0)
@@ -534,8 +616,13 @@
             pltpu.VMEM((wide, piece, 8, 128), f32),
             pltpu.VMEM((n_gy - 1, own, 8, 128), f32),
             pltpu.VMEM((chunks, 8, 128), f32),
+            pltpu.VMEM((n_gx, rows, 128), bf16),
+            pltpu.VMEM((n_gx * n_gz, rows, 128), bf16),
+            pltpu.VMEM((dirs // 128, 1, 128), f32),
+            pltpu.VMEM((n_gx * n_gy, max(own // (steps // 8), 1), 1, 128), f32),
             dma(12), dma(6), dma(6), dma(n_gx * n_gz), dma(n_gx * n_gz),
             dma(n_x), dma(n_x), dma(wide, n_gy), dma(wide, n_gy), dma(n_gy - 1), dma(n_gy - 1),
+            dma(n_gx * n_gz), dma(n_gx * n_gz), dma(n_gx * n_gy), dma(n_gx * n_gy),
             dma(n_gy - 1), dma(n_gy - 1), dma(wide, n_gy), dma(wide, n_gy), dma(n_x, n_gy), dma(n_x, n_gy),
         ],
         compiler_params=pltpu.CompilerParams(
@@ -554,7 +641,7 @@
     e_next, h_next, poles_next, far = pl.pallas_call(
         hand_out,
         out_shape=tuple(jax.ShapeDtypeStruct(result.shape, f32) for result in results),
-        in_specs=[pl.BlockSpec(memory_space=pl.ANY)] * 4,
+        in_specs=[vmem] * 4,
         out_specs=(hbm,) * 4,
         scratch_shapes=[dma(4)],
     )(*results)

time: 108 us -> 38.4 us (0.36)
  Pallas kernels: 103 us -> 34.4 us
    pallas_call x1, Pallas kernels: 68.6 us -> 3.01 us  [per_device(): pl.pallas_call(hand_out, out_shape=tuple((jax.ShapeDtypeStruct(result.sha...]
    pallas_call x1, Pallas kernels: 34.4 us -> 31.4 us  [per_device(): pl.pallas_call(functools.partial(kernel, n_gx, n_gy, n_gz, cap, rows), ou...]
where the time goes in v3:
time: 38.4 us; the launch traced here: 38.2 us
  Pallas kernels  34.4 us (90%)
  local copies, waits for them, and re-layouts  3.21 us (8%)
  between operations  0.65 us (2%)
    pallas_call x1, Pallas kernels, per_device(): pl.pallas_call(functools.partial(kernel, n_gx, n_gy, n_gz, cap, rows), ou...  31.4 us
    unnamed x8, local copies, waits for them, and re-layouts  3.21 us
    pallas_call x1, Pallas kernels, per_device(): pl.pallas_call(hand_out, out_shape=tuple((jax.ShapeDtypeStruct(result.sha...  3.01 us

profile of v3, /device:TPU:0, one launch (start us, length us, event | category | flops | bytes accessed | tf_op | source)
XLA Modules:
  0.0 38.2 jit_solution(17333214377625622174)
XLA Ops:
  0.6 31.4 %shard_map.147 = (f32[3,8,16,128]{3,2,1,0:T(8,128)S(1)}, f32[3,8,16,128]{3,2,1,0:T(8,128)S(1)}, f32[32,2048]{1,0:T(8,128)S(1)}, f32[8,3,8,16,128]{4,3,2,1,0:T(8,128)S(1)}) custom-call(f32[8]{0:T(128)} %decay_hbm.1, f32[8]{0:T(128)} %gain_hbm.1, f32[3,8,16,128]{3,2,1,0:T(8,128)} %e_hbm.1, f32[3,8,16,128]{3,2,1,0:T(8,128)} %h_hbm.1, f32[8,16,128]{2,1,0:T(8,128)} %perm_hbm.1, ...), custom_call_target="tpu_custom_call" | custom-call | tf_op jit(solution)/shard_map/pallas_call | solution.py:579
  32.0 0.0 copy-start
  32.0 1.1 %copy-done = f32[8,3,8,16,128]{4,3,2,1,0:T(8,128)} copy-done((f32[8,3,8,16,128]{4,3,2,1,0:T(8,128)}, f32[8,3,8,16,128]{4,3,2,1,0:T(8,128)S(1)}, u32[]{:S(2)}) %copy-start) | copy-done | bytes 1572888
  33.2 0.0 copy-start.1
  33.2 0.7 %copy-done.1 = f32[32,2048]{1,0:T(8,128)} copy-done((f32[32,2048]{1,0:T(8,128)}, f32[32,2048]{1,0:T(8,128)S(1)}, u32[]{:S(2)}) %copy-start.1) | copy-done | bytes 262168
  33.9 0.0 copy-start.2
  33.9 0.7 %copy-done.2 = f32[3,8,16,128]{3,2,1,0:T(8,128)} copy-done((f32[3,8,16,128]{3,2,1,0:T(8,128)}, f32[3,8,16,128]{3,2,1,0:T(8,128)S(1)}, u32[]{:S(2)}) %copy-start.2) | copy-done | bytes 196632
  34.5 0.0 copy-start.3
  34.5 0.7 %copy-done.3 = f32[3,8,16,128]{3,2,1,0:T(8,128)} copy-done((f32[3,8,16,128]{3,2,1,0:T(8,128)}, f32[3,8,16,128]{3,2,1,0:T(8,128)S(1)}, u32[]{:S(2)}) %copy-start.3) | copy-done | bytes 196632
  35.2 3.0 %shard_map.148 = (f32[3,8,16,128]{3,2,1,0:T(8,128)}, f32[3,8,16,128]{3,2,1,0:T(8,128)}, f32[8,3,8,16,128]{4,3,2,1,0:T(8,128)}, f32[32,2048]{1,0:T(8,128)}) custom-call(f32[3,8,16,128]{3,2,1,0:T(8,128)} %copy-done.2, f32[3,8,16,128]{3,2,1,0:T(8,128)} %copy-done.3, f32[8,3,8,16,128]{4,3,2,1,0:T(8,128)} %copy-done, f32[32,2048]{1,0:T(8,128)} %copy-done.1), custom_call_target="tpu_custom_call" | custom-call | tf_op jit(solution)/shard_map/pallas_call | solution.py:641
Async XLA Ops:
  32.0 1.2 %copy-start = (f32[8,3,8,16,128]{4,3,2,1,0:T(8,128)}, f32[8,3,8,16,128]{4,3,2,1,0:T(8,128)S(1)}, u32[]{:S(2)}) copy-start(f32[8,3,8,16,128]{4,3,2,1,0:T(8,128)S(1)} %get-tuple-element.14.refs_2_) | copy-start | bytes 4718596
  33.2 0.7 %copy-start.1 = (f32[32,2048]{1,0:T(8,128)}, f32[32,2048]{1,0:T(8,128)S(1)}, u32[]{:S(2)}) copy-start(f32[32,2048]{1,0:T(8,128)S(1)} %get-tuple-element.15.refs_3_) | copy-start | bytes 786436
  33.9 0.7 %copy-start.2 = (f32[3,8,16,128]{3,2,1,0:T(8,128)}, f32[3,8,16,128]{3,2,1,0:T(8,128)S(1)}, u32[]{:S(2)}) copy-start(f32[3,8,16,128]{3,2,1,0:T(8,128)S(1)} %get-tuple-element.12.refs_0_) | copy-start | bytes 589828
  34.5 0.7 %copy-start.3 = (f32[3,8,16,128]{3,2,1,0:T(8,128)}, f32[3,8,16,128]{3,2,1,0:T(8,128)S(1)}, u32[]{:S(2)}) copy-start(f32[3,8,16,128]{3,2,1,0:T(8,128)S(1)} %get-tuple-element.13.refs_1_) | copy-start | bytes 589828

commit v4 on v3

--- a/solution.py
+++ b/solution.py
@@ -24,14 +24,14 @@
 def kernel(
     n_gx, n_gy, n_gz, cap, rows,
     decay_hbm, gain_hbm, e_hbm, h_hbm, perm_hbm, mask_hbm, cells_hbm, owners_hbm, hist_hbm,
-    table_hbm, poles_hbm, steer_hbm,
+    table_hbm, last_hbm, poles_hbm, steer_hbm,
     e_out, h_out, far_out, poles_out,
-    decay, gain, e_ref, h_ref, perm_ref, mask_ref, cells_ref, own_ref, hist_ref, table_ref,
+    decay, gain, e_ref, h_ref, perm_ref, mask_ref, cells_ref, own_ref, hist_ref, table_ref, last_ref,
     poles, steer, edge_j, edge_k, got_i, got_j, got_k,
-    low_j, low_k, from_i, from_j, from_k, compact, tile, part, got_1, got_2, got_3, full, new_out, new_in, new_row, got_row,
+    low_j, low_k, from_i, from_j, from_k, compact, tile, part, got_1, got_2, got_3, full, new_out, new_in, new_row, got_row, row_all,
     local_sem, halo_send, halo_recv, tile_send, tile_recv,
     core_send, core_recv, mid_send, mid_recv, end_send, end_recv,
-    new_send, new_recv, row_send, row_recv, back_z_send, back_z_recv, back_x_send, back_x_recv, back_c_send, back_c_recv,
+    new_send, new_recv, row_send, row_recv, all_send, all_recv, back_z_send, back_z_recv, back_x_send, back_x_recv, back_c_send, back_c_recv,
 ):
     gx, gy, gz = lax.axis_index("gx"), lax.axis_index("gy"), lax.axis_index("gz")
     n_x = n_gx // 2
@@ -47,19 +47,6 @@
     width = piece // t_blocks * 128
     early = own % t_blocks == 0 and rows == cap
 
-    block = gx * n_gy + gy
-    loads = [
-        pltpu.make_async_copy(source, target, local_sem.at[index])
-        for index, (source, target) in enumerate((
-            (e_hbm, e_ref), (h_hbm, h_ref), (owners_hbm, own_ref), (hist_hbm, hist_ref),
-            (cells_hbm, cells_ref), (steer_hbm, steer), (poles_hbm, poles), (perm_hbm, perm_ref),
-            (mask_hbm, mask_ref), (decay_hbm, decay), (gain_hbm, gain),
-            (table_hbm.at[block], table_ref),
-        ))
-    ]
-    for load in loads:
-        load.start()
-
     barrier = pltpu.get_barrier_semaphore()
     partners = 0
     for da in range(n_gx):
@@ -73,6 +60,19 @@
             peer = (lax.rem(gx + da, n_gx), lax.rem(gy + dw, n_gy), gz)
             pl.semaphore_signal(barrier, inc=1, device_id=peer, device_id_type=MESH)
             partners += 1
+
+    block = gx * n_gy + gy
+    loads = [
+        pltpu.make_async_copy(source, target, local_sem.at[index])
+        for index, (source, target) in enumerate((
+            (e_hbm, e_ref), (h_hbm, h_ref), (owners_hbm, own_ref), (hist_hbm, hist_ref),
+            (cells_hbm, cells_ref), (steer_hbm, steer), (poles_hbm, poles), (perm_hbm, perm_ref),
+            (mask_hbm, mask_ref), (decay_hbm, decay), (gain_hbm, gain),
+            (table_hbm.at[block], table_ref), (last_hbm.at[block], last_ref),
+        ))
+    ]
+    for load in loads:
+        load.start()
 
     def remote(src, dst, send, recv, peer):
         return pltpu.make_async_remote_copy(
@@ -264,6 +264,7 @@
     def first_half(copies):
         loads[5].wait()
         loads[11].wait()
+        loads[12].wait()
         for copy in copies:
             copy.wait_recv()
 
@@ -425,14 +426,6 @@
         third[dw].wait_recv()
         total = total + got_3[dw - 1]
     full[pl.ds(mine, own)] = total
-    if early:
-        added = new_row[pl.ds(mine // t_blocks, count_d)]
-        for index in rows_out:
-            rows_out[index].wait_recv()
-            added = added + got_row[index]
-        for index in range(count_d):
-            full[mine + (index + 1) * t_blocks - 1, 7:8, :] += added[index]
-
     def transform(start, many):
         for index in range(many // t_blocks):
             at = start // t_blocks + index
@@ -441,8 +434,10 @@
                 at = pl.multiple_of(at * 128, 128)
             else:
                 at = at * 128
+            high = values.astype(jnp.bfloat16)
+            low = (values - high.astype(jnp.float32)).astype(jnp.bfloat16)
             far_out[:, pl.ds(at, 128)] = jnp.dot(
-                table_ref[...], values, precision=lax.Precision.HIGHEST,
+                table_ref[...], jnp.concatenate([high, low, high], axis=0),
                 preferred_element_type=jnp.float32,
             )
 
@@ -482,6 +477,27 @@
     to_mid(mine, 0)
     to_core(mine, 0, 0)
     arrived(mine)
+    rows_back = []
+    if early:
+        mine_d = mine // t_blocks
+        added = new_row[pl.ds(mine_d, count_d)]
+        for index in rows_out:
+            rows_out[index].wait_recv()
+            added = added + got_row[index]
+        row_all[pl.ds(mine_d, count_d)] = added
+        for da in range(n_gx):
+            for dw in range(n_gy):
+                if da or dw:
+                    index = da * n_gy + dw
+                    block = row_all.at[pl.ds(mine_d, count_d)]
+                    rows_back.append(
+                        begin(
+                            remote(
+                                block, block, all_send.at[index], all_recv.at[index],
+                                (lax.rem(gx + da, n_gx), lax.rem(gy + dw, n_gy), gz),
+                            )
+                        )
+                    )
     for dw in range(1, n_gy):
         long[dw].wait_recv()
         start = base + lax.rem(gy + n_gy - dw, n_gy) * own
@@ -506,7 +522,13 @@
                 + lax.rem(mid + n_x - dq, n_x) * piece
                 + lax.rem(gy + n_gy - dw, n_gy) * own
             )
-    if not early:
+    if early:
+        for copy in rows_back:
+            copy.wait_recv()
+        last_step = last_ref[...]
+        for index in range(chunks // t_blocks):
+            far_out[:, index * 128 : (index + 1) * 128] += last_step * row_all[index]
+    else:
         transform(0, chunks)
 
     for copy in sends + tile_copies + (new_copies if early else []):
@@ -565,6 +587,10 @@
 
     table = spectral_rows(FREQS, FREQS, steps)
     table = table.reshape(2, blocks, mine, steps).transpose(1, 0, 2, 3).reshape(blocks, 2 * mine, steps)
+    high = table.astype(jnp.bfloat16)
+    low = (table - high.astype(np.float32)).astype(jnp.bfloat16)
+    split = np.concatenate([high, high, low], axis=2)
+    last = np.broadcast_to(table[:, :, -1:], table.shape[:2] + (128,)).copy()
     hist = jnp.transpose(history, (1, 2, 0))
 
     chunks = steps // 8 * (dirs // 128)
@@ -584,7 +610,7 @@
             jax.ShapeDtypeStruct((2 * mine, dirs), f32),
             jax.ShapeDtypeStruct(poles.shape, f32),
         ),
-        in_specs=[hbm] * 12,
+        in_specs=[hbm] * 13,
         out_specs=(vmem, vmem, vmem, vmem),
         scratch_shapes=[
             pltpu.SMEM(pole_decay.shape, f32),
@@ -596,7 +622,8 @@
             pltpu.VMEM((1, count), jnp.int32),
             pltpu.VMEM((1, count), jnp.int32),
             pltpu.VMEM(hist.shape, bf16),
-            pltpu.VMEM(table.shape[1:], f32),
+            pltpu.VMEM(split.shape[1:], bf16),
+            pltpu.VMEM(last.shape[1:], f32),
             pltpu.VMEM(poles.shape, f32),
             pltpu.VMEM(steering.shape, bf16),
             pltpu.VMEM((2, span_x, span_z), f32),
@@ -620,10 +647,11 @@
             pltpu.VMEM((n_gx * n_gz, rows, 128), bf16),
             pltpu.VMEM((dirs // 128, 1, 128), f32),
             pltpu.VMEM((n_gx * n_gy, max(own // (steps // 8), 1), 1, 128), f32),
-            dma(12), dma(6), dma(6), dma(n_gx * n_gz), dma(n_gx * n_gz),
+            pltpu.VMEM((dirs // 128, 1, 128), f32),
+            dma(13), dma(6), dma(6), dma(n_gx * n_gz), dma(n_gx * n_gz),
             dma(n_x), dma(n_x), dma(wide, n_gy), dma(wide, n_gy), dma(n_gy - 1), dma(n_gy - 1),
             dma(n_gx * n_gz), dma(n_gx * n_gz), dma(n_gx * n_gy), dma(n_gx * n_gy),
-            dma(n_gy - 1), dma(n_gy - 1), dma(wide, n_gy), dma(wide, n_gy), dma(n_x, n_gy), dma(n_x, n_gy),
+            dma(n_gx * n_gy), dma(n_gx * n_gy), dma(n_gy - 1), dma(n_gy - 1), dma(wide, n_gy), dma(wide, n_gy), dma(n_x, n_gy), dma(n_x, n_gy),
         ],
         compiler_params=pltpu.CompilerParams(
             collective_id=0, has_side_effects=True, vmem_limit_bytes=32 * 1024 * 1024
@@ -633,7 +661,7 @@
             pltpu.with_memory_space_constraint(operand, pltpu.HBM)
             for operand in (
                 pole_decay, pole_gain, e_field, h_field, permittivity, wall_mask, face_cells.reshape(1, count),
-                owners.reshape(1, count), hist, jnp.asarray(table), poles, steering,
+                owners.reshape(1, count), hist, jnp.asarray(split), jnp.asarray(last), poles, steering,
             )
         )
     )
@@ -644,6 +672,7 @@
         in_specs=[vmem] * 4,
         out_specs=(hbm,) * 4,
         scratch_shapes=[dma(4)],
+        compiler_params=pltpu.CompilerParams(vmem_limit_bytes=8 * 1024 * 1024),
     )(*results)
     return (e_next, h_next, poles_next, far.reshape(2, mine, dirs))
 

time: 38.4 us -> 31.9 us (0.83)
  Pallas kernels: 34.4 us -> 31.1 us
  local copies, waits for them, and re-layouts: 3.21 us -> 0 us
    unnamed x8 -> x0, local copies, waits for them, and re-layouts: 3.21 us -> none
    pallas_call x1, Pallas kernels: 31.4 us -> 29.7 us  [per_device(): pl.pallas_call(functools.partial(kernel, n_gx, n_gy, n_gz, cap, rows), ou...]
    pallas_call x1, Pallas kernels: 3.01 us -> 1.39 us  [per_device(): pl.pallas_call(hand_out, out_shape=tuple((jax.ShapeDtypeStruct(result.sha...]
where the time goes in v4:
time: 31.9 us; the launch traced here: 31.7 us
  Pallas kernels  31.1 us (97%)
  between operations  0.64 us (2%)
    pallas_call x1, Pallas kernels, per_device(): pl.pallas_call(functools.partial(kernel, n_gx, n_gy, n_gz, cap, rows), ou...  29.7 us
    pallas_call x1, Pallas kernels, per_device(): pl.pallas_call(hand_out, out_shape=tuple((jax.ShapeDtypeStruct(result.sha...  1.39 us

profile of v4, /device:TPU:0, one launch (start us, length us, event | category | flops | bytes accessed | tf_op | source)
XLA Modules:
  0.0 31.7 jit_solution(8093598218841205444)
XLA Ops:
  0.6 29.7 %shard_map.156 = (f32[3,8,16,128]{3,2,1,0:T(8,128)S(1)}, f32[3,8,16,128]{3,2,1,0:T(8,128)S(1)}, f32[32,2048]{1,0:T(8,128)S(1)}, f32[8,3,8,16,128]{4,3,2,1,0:T(8,128)S(1)}) custom-call(f32[8]{0:T(128)} %decay_hbm.1, f32[8]{0:T(128)} %gain_hbm.1, f32[3,8,16,128]{3,2,1,0:T(8,128)} %e_hbm.1, f32[3,8,16,128]{3,2,1,0:T(8,128)} %h_hbm.1, f32[8,16,128]{2,1,0:T(8,128)} %perm_hbm.1, ...), custom_call_target="tpu_custom_call" | custom-call | tf_op jit(solution)/shard_map/pallas_call | solution.py:605
  30.3 1.4 %shard_map.157 = (f32[3,8,16,128]{3,2,1,0:T(8,128)}, f32[3,8,16,128]{3,2,1,0:T(8,128)}, f32[8,3,8,16,128]{4,3,2,1,0:T(8,128)}, f32[32,2048]{1,0:T(8,128)}) custom-call(f32[3,8,16,128]{3,2,1,0:T(8,128)S(1)} %get-tuple-element.12.refs_0_, f32[3,8,16,128]{3,2,1,0:T(8,128)S(1)} %get-tuple-element.13.refs_1_, ...), custom_call_target="tpu_custom_call" | custom-call | tf_op jit(solution)/shard_map/pallas_call | solution.py:669

commit v5 on v4

--- a/solution.py
+++ b/solution.py
@@ -65,7 +65,7 @@
     loads = [
         pltpu.make_async_copy(source, target, local_sem.at[index])
         for index, (source, target) in enumerate((
-            (e_hbm, e_ref), (h_hbm, h_ref), (owners_hbm, own_ref), (hist_hbm, hist_ref),
+            (owners_hbm, own_ref), (hist_hbm, hist_ref), (e_hbm, e_ref), (h_hbm, h_ref),
             (cells_hbm, cells_ref), (steer_hbm, steer), (poles_hbm, poles), (perm_hbm, perm_ref),
             (mask_hbm, mask_ref), (decay_hbm, decay), (gain_hbm, gain),
             (table_hbm.at[block], table_ref), (last_hbm.at[block], last_ref),
@@ -98,14 +98,7 @@
     down_j = remote(low_j, from_j, halo_send.at[4], halo_recv.at[4], (gx, gy + 1, gz))
     down_k = remote(low_k, from_k, halo_send.at[5], halo_recv.at[5], (gx, gy, gz + 1))
 
-    loads[0].wait()
-    edge_k[0:1] = column(e_ref[0], 0)
-    edge_k[1:2] = column(e_ref[1], 0)
-    edge_k[2:8] = jnp.zeros((6, flat[0]), jnp.float32)
-    edge_j[0] = e_ref[0, :, 0, :]
-    edge_j[1] = e_ref[2, :, 0, :]
-
-    for load in loads[1:5]:
+    for load in loads[:2]:
         load.wait()
     sample = lax.broadcasted_iota(jnp.int32, (count, count), 0)
     other_sample = lax.broadcasted_iota(jnp.int32, (count, count), 1)
@@ -131,11 +124,17 @@
         samples += jnp.dot(hist_ref[comp], spot, preferred_element_type=jnp.float32)
     me = gz * n_gx + gx
 
-    def send(values, source, target, send_sem, recv_sem):
+    def pack(values, source):
         packed = jnp.dot(
             place, values.astype(jnp.bfloat16), preferred_element_type=jnp.float32
         ).astype(jnp.bfloat16)
         source[...] = packed.reshape(source.shape)
+
+    def send(values, source, target, send_sem, recv_sem):
+        pack(values, source)
+        return launch(source, target, send_sem, recv_sem)
+
+    def launch(source, target, send_sem, recv_sem):
         copies = []
         for da in range(n_gx):
             for dz in range(n_gz):
@@ -154,7 +153,18 @@
     def send_tiles():
         return send(samples, compact, tile, tile_send, tile_recv)
 
+    if early:
+        pack(samples, compact)
+    loads[2].wait()
+    edge_k[0:1] = column(e_ref[0], 0)
+    edge_k[1:2] = column(e_ref[1], 0)
+    edge_k[2:8] = jnp.zeros((6, flat[0]), jnp.float32)
+    edge_j[0] = e_ref[0, :, 0, :]
+    edge_j[1] = e_ref[2, :, 0, :]
+
     pl.semaphore_wait(barrier, partners)
+    if early:
+        tile_copies = launch(compact, tile, tile_send, tile_recv)
 
     @pl.when(gz > 0)
     def _():
@@ -168,8 +178,8 @@
     def _():
         up_j.start()
 
-    if early:
-        tile_copies = send_tiles()
+    for load in loads[3:5]:
+        load.wait()
 
     @pl.when(gx == n_gx - 1)
     def _():
@@ -259,7 +269,7 @@
         return copy
 
     other = (mid * 2 + 1 - core, gy, gz)
-    second = {}
+    first, second = {}, {}
 
     def first_half(copies):
         loads[5].wait()
@@ -292,7 +302,6 @@
                     :, block * 128 : (block + 1) * 128
                 ].reshape(t_blocks, 8, 128)
 
-        first = {}
         for dq in order_x:
             to = lax.rem(mid + dq, n_x)
             start = (1 - core) * half + to * piece
@@ -305,6 +314,7 @@
             )
         for dq in order_x:
             fill(core * half + lax.rem(mid + dq, n_x) * piece)
+    def pass_on():
         for dq in order_x:
             to = lax.rem(mid + dq, n_x)
             start = core * half + to * piece
@@ -378,22 +388,8 @@
     else:
         tile_copies = send_tiles()
         first_half(tile_copies)
-    base = core * half + mid * piece
-    third = {}
-    for dw in order_z:
-        to = lax.rem(gy + dw, n_gy)
-        at = to * own
-        for dq in range(1, n_x):
-            second[dq, dw].wait_recv()
-            part[pl.ds(base + at, own)] += got_2[dq - 1, pl.ds(at, own)]
-        if dw:
-            third[dw] = begin(
-                remote(
-                    part.at[pl.ds(base + at, own)], got_3.at[dw - 1],
-                    end_send.at[dw - 1], end_recv.at[dw - 1], (gx, to, gz),
-                )
-            )
-    mine = base + gy * own
+    pass_on()
+
     rows_out = {}
     if early:
         for copy in new_copies:
@@ -421,6 +417,22 @@
                             row_send.at[index], row_recv.at[index], (to_x, to_y, gz),
                         )
                     )
+    base = core * half + mid * piece
+    third = {}
+    for dw in order_z:
+        to = lax.rem(gy + dw, n_gy)
+        at = to * own
+        for dq in range(1, n_x):
+            second[dq, dw].wait_recv()
+            part[pl.ds(base + at, own)] += got_2[dq - 1, pl.ds(at, own)]
+        if dw:
+            third[dw] = begin(
+                remote(
+                    part.at[pl.ds(base + at, own)], got_3.at[dw - 1],
+                    end_send.at[dw - 1], end_recv.at[dw - 1], (gx, to, gz),
+                )
+            )
+    mine = base + gy * own
     total = part[pl.ds(mine, own)]
     for dw in range(1, n_gy):
         third[dw].wait_recv()
@@ -560,8 +572,13 @@
 
 
 def hand_out(*refs):
+    sources, targets, sems = refs[:4], refs[4:8], refs[8]
+    pairs = [(sources[index], targets[index]) for index in (0, 1, 3)]
+    for pole in range(sources[2].shape[0]):
+        pairs.append((sources[2].at[pole], targets[2].at[pole]))
     copies = [
-        pltpu.make_async_copy(refs[index], refs[4 + index], refs[8].at[index]) for index in range(4)
+        pltpu.make_async_copy(source, target, sems.at[index])
+        for index, (source, target) in enumerate(pairs)
     ]
     for copy in copies:
         copy.start()
@@ -671,7 +688,7 @@
         out_shape=tuple(jax.ShapeDtypeStruct(result.shape, f32) for result in results),
         in_specs=[vmem] * 4,
         out_specs=(hbm,) * 4,
-        scratch_shapes=[dma(4)],
+        scratch_shapes=[dma(3 + poles.shape[0])],
         compiler_params=pltpu.CompilerParams(vmem_limit_bytes=8 * 1024 * 1024),
     )(*results)
     return (e_next, h_next, poles_next, far.reshape(2, mine, dirs))

time: 31.9 us -> 34.5 us (1.082)
  Pallas kernels: 31.1 us -> 33.7 us
    pallas_call x1, Pallas kernels: 29.7 us -> 32.2 us  [per_device(): pl.pallas_call(functools.partial(kernel, n_gx, n_gy, n_gz, cap, rows), ou...]
where the time goes in v5:
time: 34.5 us; the launch traced here: 34.3 us
  Pallas kernels  33.7 us (98%)
  between operations  0.64 us (2%)
    pallas_call x1, Pallas kernels, per_device(): pl.pallas_call(functools.partial(kernel, n_gx, n_gy, n_gz, cap, rows), ou...  32.2 us
    pallas_call x1, Pallas kernels, per_device(): pl.pallas_call(hand_out, out_shape=tuple((jax.ShapeDtypeStruct(result.sha...  1.44 us

profile of v5, /device:TPU:0, one launch (start us, length us, event | category | flops | bytes accessed | tf_op | source)
XLA Modules:
  0.0 34.3 jit_solution(17270825301390229894)
XLA Ops:
  0.6 32.2 %shard_map.156 = (f32[3,8,16,128]{3,2,1,0:T(8,128)S(1)}, f32[3,8,16,128]{3,2,1,0:T(8,128)S(1)}, f32[32,2048]{1,0:T(8,128)S(1)}, f32[8,3,8,16,128]{4,3,2,1,0:T(8,128)S(1)}) custom-call(f32[8]{0:T(128)} %decay_hbm.1, f32[8]{0:T(128)} %gain_hbm.1, f32[3,8,16,128]{3,2,1,0:T(8,128)} %e_hbm.1, f32[3,8,16,128]{3,2,1,0:T(8,128)} %h_hbm.1, f32[8,16,128]{2,1,0:T(8,128)} %perm_hbm.1, ...), custom_call_target="tpu_custom_call" | custom-call | tf_op jit(solution)/shard_map/pallas_call | solution.py:622
  32.9 1.4 %shard_map.157 = (f32[3,8,16,128]{3,2,1,0:T(8,128)}, f32[3,8,16,128]{3,2,1,0:T(8,128)}, f32[8,3,8,16,128]{4,3,2,1,0:T(8,128)}, f32[32,2048]{1,0:T(8,128)}) custom-call(f32[3,8,16,128]{3,2,1,0:T(8,128)S(1)} %get-tuple-element.12.refs_0_, f32[3,8,16,128]{3,2,1,0:T(8,128)S(1)} %get-tuple-element.13.refs_1_, ...), custom_call_target="tpu_custom_call" | custom-call | tf_op jit(solution)/shard_map/pallas_call | solution.py:686

commit v6 on v5

--- a/solution.py
+++ b/solution.py
@@ -219,45 +219,6 @@
 
     def prev_k(field, halo):
         return jnp.where(at_k == 0, spread(halo), pltpu.roll(field, 1, 2))
-
-    @pl.when(gx < n_gx - 1)
-    def _():
-        up_i.wait_recv()
-
-    @pl.when(gy < n_gy - 1)
-    def _():
-        up_j.wait_recv()
-
-    @pl.when(gz < n_gz - 1)
-    def _():
-        up_k.wait_recv()
-
-    ex, ey, ez = e_ref[0], e_ref[1], e_ref[2]
-    ey_i = jnp.concatenate([ey[1:], got_i[0][None]], axis=0)
-    ez_i = jnp.concatenate([ez[1:], got_i[1][None]], axis=0)
-    mag_x = h_ref[0] - 0.5 * (next_j(ez, got_j[1]) - ez - (next_k(ey, got_k[1:2]) - ey))
-    h_out[0] = mag_x
-    mag_y = h_ref[1] - 0.5 * (next_k(ex, got_k[0:1]) - ex - (ez_i - ez))
-    h_out[1] = mag_y
-    mag_z = h_ref[2] - 0.5 * (ey_i - ey - (next_j(ex, got_j[0]) - ex))
-    h_out[2] = mag_z
-
-    @pl.when(gx < n_gx - 1)
-    def _():
-        down_i.start()
-
-    @pl.when(gz < n_gz - 1)
-    def _():
-        low_k[0:1] = column(h_out[0], span_z - 1)
-        low_k[1:2] = column(h_out[1], span_z - 1)
-        low_k[2:8] = jnp.zeros((6, flat[0]), jnp.float32)
-        down_k.start()
-
-    @pl.when(gy < n_gy - 1)
-    def _():
-        low_j[0] = h_out[0, :, span_y - 1, :]
-        low_j[1] = h_out[2, :, span_y - 1, :]
-        down_j.start()
 
     order_x = list(range(1, n_x)) + [0]
     order_z = list(range(1, n_gy)) + [0]
@@ -333,6 +294,48 @@
     if early:
         first_half(tile_copies)
 
+    @pl.when(gx < n_gx - 1)
+    def _():
+        up_i.wait_recv()
+
+    @pl.when(gy < n_gy - 1)
+    def _():
+        up_j.wait_recv()
+
+    @pl.when(gz < n_gz - 1)
+    def _():
+        up_k.wait_recv()
+
+    ex, ey, ez = e_ref[0], e_ref[1], e_ref[2]
+    ey_i = jnp.concatenate([ey[1:], got_i[0][None]], axis=0)
+    ez_i = jnp.concatenate([ez[1:], got_i[1][None]], axis=0)
+    mag_x = h_ref[0] - 0.5 * (next_j(ez, got_j[1]) - ez - (next_k(ey, got_k[1:2]) - ey))
+    h_out[0] = mag_x
+    mag_y = h_ref[1] - 0.5 * (next_k(ex, got_k[0:1]) - ex - (ez_i - ez))
+    h_out[1] = mag_y
+    mag_z = h_ref[2] - 0.5 * (ey_i - ey - (next_j(ex, got_j[0]) - ex))
+    h_out[2] = mag_z
+
+    @pl.when(gx < n_gx - 1)
+    def _():
+        down_i.start()
+
+    @pl.when(gz < n_gz - 1)
+    def _():
+        low_k[0:1] = column(h_out[0], span_z - 1)
+        low_k[1:2] = column(h_out[1], span_z - 1)
+        low_k[2:8] = jnp.zeros((6, flat[0]), jnp.float32)
+        down_k.start()
+
+    @pl.when(gy < n_gy - 1)
+    def _():
+        low_j[0] = h_out[0, :, span_y - 1, :]
+        low_j[1] = h_out[2, :, span_y - 1, :]
+        down_j.start()
+
+    if early:
+        pass_on()
+
     for load in loads[6:11]:
         load.wait()
 
@@ -358,7 +361,8 @@
     )
     wall = mask_ref[...] == 1
     half_eps = 0.5 / perm_ref[...]
-    for comp in range(3):
+
+    def advance(comp):
         drive = drives[comp]
         total = None
         for pole in range(poles.shape[0]):
@@ -366,6 +370,10 @@
             poles_out[pole, comp] = state
             total = state if total is None else total + state
         e_out[comp] = jnp.where(wall, total, e_ref[comp] + half_eps * drive)
+
+    advance(0)
+    advance(1)
+
 
     cell = upright(cells_ref[...])
     row_hot = (
@@ -388,8 +396,24 @@
     else:
         tile_copies = send_tiles()
         first_half(tile_copies)
-    pass_on()
-
+        pass_on()
+
+    base = core * half + mid * piece
+    third = {}
+    for dw in order_z:
+        to = lax.rem(gy + dw, n_gy)
+        at = to * own
+        for dq in range(1, n_x):
+            second[dq, dw].wait_recv()
+            part[pl.ds(base + at, own)] += got_2[dq - 1, pl.ds(at, own)]
+        if dw:
+            third[dw] = begin(
+                remote(
+                    part.at[pl.ds(base + at, own)], got_3.at[dw - 1],
+                    end_send.at[dw - 1], end_recv.at[dw - 1], (gx, to, gz),
+                )
+            )
+    mine = base + gy * own
     rows_out = {}
     if early:
         for copy in new_copies:
@@ -417,22 +441,6 @@
                             row_send.at[index], row_recv.at[index], (to_x, to_y, gz),
                         )
                     )
-    base = core * half + mid * piece
-    third = {}
-    for dw in order_z:
-        to = lax.rem(gy + dw, n_gy)
-        at = to * own
-        for dq in range(1, n_x):
-            second[dq, dw].wait_recv()
-            part[pl.ds(base + at, own)] += got_2[dq - 1, pl.ds(at, own)]
-        if dw:
-            third[dw] = begin(
-                remote(
-                    part.at[pl.ds(base + at, own)], got_3.at[dw - 1],
-                    end_send.at[dw - 1], end_recv.at[dw - 1], (gx, to, gz),
-                )
-            )
-    mine = base + gy * own
     total = part[pl.ds(mine, own)]
     for dw in range(1, n_gy):
         third[dw].wait_recv()
@@ -489,6 +497,7 @@
     to_mid(mine, 0)
     to_core(mine, 0, 0)
     arrived(mine)
+    advance(2)
     rows_back = []
     if early:
         mine_d = mine // t_blocks
@@ -573,9 +582,7 @@
 
 def hand_out(*refs):
     sources, targets, sems = refs[:4], refs[4:8], refs[8]
-    pairs = [(sources[index], targets[index]) for index in (0, 1, 3)]
-    for pole in range(sources[2].shape[0]):
-        pairs.append((sources[2].at[pole], targets[2].at[pole]))
+    pairs = zip(sources, targets)
     copies = [
         pltpu.make_async_copy(source, target, sems.at[index])
         for index, (source, target) in enumerate(pairs)
@@ -688,7 +695,7 @@
         out_shape=tuple(jax.ShapeDtypeStruct(result.shape, f32) for result in results),
         in_specs=[vmem] * 4,
         out_specs=(hbm,) * 4,
-        scratch_shapes=[dma(3 + poles.shape[0])],
+        scratch_shapes=[dma(4)],
         compiler_params=pltpu.CompilerParams(vmem_limit_bytes=8 * 1024 * 1024),
     )(*results)
     return (e_next, h_next, poles_next, far.reshape(2, mine, dirs))

time: 34.5 us -> 31.7 us (0.919)
  Pallas kernels: 33.7 us -> 30.9 us
    pallas_call x1, Pallas kernels: 32.2 us -> 29.5 us  [per_device(): pl.pallas_call(functools.partial(kernel, n_gx, n_gy, n_gz, cap, rows), ou...]
where the time goes in v6:
time: 31.7 us; the launch traced here: 31.6 us
  Pallas kernels  30.9 us (97%)
  between operations  0.64 us (2%)
    pallas_call x1, Pallas kernels, per_device(): pl.pallas_call(functools.partial(kernel, n_gx, n_gy, n_gz, cap, rows), ou...  29.5 us
    pallas_call x1, Pallas kernels, per_device(): pl.pallas_call(hand_out, out_shape=tuple((jax.ShapeDtypeStruct(result.sha...  1.39 us

profile of v6, /device:TPU:0, one launch (start us, length us, event | category | flops | bytes accessed | tf_op | source)
XLA Modules:
  0.0 31.6 jit_solution(10474441341311241381)
XLA Ops:
  0.6 29.5 %shard_map.156 = (f32[3,8,16,128]{3,2,1,0:T(8,128)S(1)}, f32[3,8,16,128]{3,2,1,0:T(8,128)S(1)}, f32[32,2048]{1,0:T(8,128)S(1)}, f32[8,3,8,16,128]{4,3,2,1,0:T(8,128)S(1)}) custom-call(f32[8]{0:T(128)} %decay_hbm.1, f32[8]{0:T(128)} %gain_hbm.1, f32[3,8,16,128]{3,2,1,0:T(8,128)} %e_hbm.1, f32[3,8,16,128]{3,2,1,0:T(8,128)} %h_hbm.1, f32[8,16,128]{2,1,0:T(8,128)} %perm_hbm.1, ...), custom_call_target="tpu_custom_call" | custom-call | tf_op jit(solution)/shard_map/pallas_call | solution.py:629
  30.2 1.4 %shard_map.157 = (f32[3,8,16,128]{3,2,1,0:T(8,128)}, f32[3,8,16,128]{3,2,1,0:T(8,128)}, f32[8,3,8,16,128]{4,3,2,1,0:T(8,128)}, f32[32,2048]{1,0:T(8,128)}) custom-call(f32[3,8,16,128]{3,2,1,0:T(8,128)S(1)} %get-tuple-element.12.refs_0_, f32[3,8,16,128]{3,2,1,0:T(8,128)S(1)} %get-tuple-element.13.refs_1_, ...), custom_call_target="tpu_custom_call" | custom-call | tf_op jit(solution)/shard_map/pallas_call | solution.py:693

commit v7 on v6

--- a/solution.py
+++ b/solution.py
@@ -414,6 +414,62 @@
                 )
             )
     mine = base + gy * own
+    total = part[pl.ds(mine, own)]
+    for dw in range(1, n_gy):
+        third[dw].wait_recv()
+        total = total + got_3[dw - 1]
+    full[pl.ds(mine, own)] = total
+    def transform(start, many):
+        for index in range(many // t_blocks):
+            at = start // t_blocks + index
+            values = full[pl.ds(at * t_blocks, t_blocks)].reshape(steps, 128)
+            if not isinstance(at, int):
+                at = pl.multiple_of(at * 128, 128)
+            else:
+                at = at * 128
+            high = values.astype(jnp.bfloat16)
+            low = (values - high.astype(jnp.float32)).astype(jnp.bfloat16)
+            far_out[:, pl.ds(at, 128)] = jnp.dot(
+                table_ref[...], jnp.concatenate([high, low, high], axis=0),
+                preferred_element_type=jnp.float32,
+            )
+
+    def arrived(start):
+        if early:
+            transform(start, own)
+
+    last = {}
+
+    def to_core(start, dq, dw):
+        block = full.at[pl.ds(start, own)]
+        last[dq, dw] = begin(
+            remote(block, block, back_c_send.at[dq, dw], back_c_recv.at[dq, dw], other)
+        )
+
+    wide = {}
+
+    def to_mid(start, dw):
+        block = full.at[pl.ds(start, own)]
+        for dq in range(1, n_x):
+            wide[dq, dw] = begin(
+                remote(
+                    block, block, back_x_send.at[dq - 1, dw], back_x_recv.at[dq - 1, dw],
+                    (lax.rem(mid + dq, n_x) * 2 + core, gy, gz),
+                )
+            )
+
+    long = {}
+    for dw in range(1, n_gy):
+        block = full.at[pl.ds(mine, own)]
+        long[dw] = begin(
+            remote(
+                block, block, back_z_send.at[dw - 1], back_z_recv.at[dw - 1],
+                (gx, lax.rem(gy + dw, n_gy), gz),
+            )
+        )
+    to_mid(mine, 0)
+    to_core(mine, 0, 0)
+    arrived(mine)
     rows_out = {}
     if early:
         for copy in new_copies:
@@ -441,62 +497,12 @@
                             row_send.at[index], row_recv.at[index], (to_x, to_y, gz),
                         )
                     )
-    total = part[pl.ds(mine, own)]
     for dw in range(1, n_gy):
-        third[dw].wait_recv()
-        total = total + got_3[dw - 1]
-    full[pl.ds(mine, own)] = total
-    def transform(start, many):
-        for index in range(many // t_blocks):
-            at = start // t_blocks + index
-            values = full[pl.ds(at * t_blocks, t_blocks)].reshape(steps, 128)
-            if not isinstance(at, int):
-                at = pl.multiple_of(at * 128, 128)
-            else:
-                at = at * 128
-            high = values.astype(jnp.bfloat16)
-            low = (values - high.astype(jnp.float32)).astype(jnp.bfloat16)
-            far_out[:, pl.ds(at, 128)] = jnp.dot(
-                table_ref[...], jnp.concatenate([high, low, high], axis=0),
-                preferred_element_type=jnp.float32,
-            )
-
-    def arrived(start):
-        if early:
-            transform(start, own)
-
-    last = {}
-
-    def to_core(start, dq, dw):
-        block = full.at[pl.ds(start, own)]
-        last[dq, dw] = begin(
-            remote(block, block, back_c_send.at[dq, dw], back_c_recv.at[dq, dw], other)
-        )
-
-    wide = {}
-
-    def to_mid(start, dw):
-        block = full.at[pl.ds(start, own)]
-        for dq in range(1, n_x):
-            wide[dq, dw] = begin(
-                remote(
-                    block, block, back_x_send.at[dq - 1, dw], back_x_recv.at[dq - 1, dw],
-                    (lax.rem(mid + dq, n_x) * 2 + core, gy, gz),
-                )
-            )
-
-    long = {}
-    for dw in range(1, n_gy):
-        block = full.at[pl.ds(mine, own)]
-        long[dw] = begin(
-            remote(
-                block, block, back_z_send.at[dw - 1], back_z_recv.at[dw - 1],
-                (gx, lax.rem(gy + dw, n_gy), gz),
-            )
-        )
-    to_mid(mine, 0)
-    to_core(mine, 0, 0)
-    arrived(mine)
+        long[dw].wait_recv()
+        start = base + lax.rem(gy + n_gy - dw, n_gy) * own
+        to_mid(start, dw)
+        to_core(start, 0, dw)
+        arrived(start)
     advance(2)
     rows_back = []
     if early:
@@ -519,12 +525,6 @@
                             )
                         )
                     )
-    for dw in range(1, n_gy):
-        long[dw].wait_recv()
-        start = base + lax.rem(gy + n_gy - dw, n_gy) * own
-        to_mid(start, dw)
-        to_core(start, 0, dw)
-        arrived(start)
     for dw in range(n_gy):
         for dq in range(1, n_x):
             wide[dq, dw].wait_recv()

time: 31.7 us -> 31.8 us (level)
  no operation moved by 1% of the time
where the time goes in v7:
time: 31.8 us; the launch traced here: 31.6 us
  Pallas kernels  31 us (97%)
  between operations  0.64 us (2%)
    pallas_call x1, Pallas kernels, per_device(): pl.pallas_call(functools.partial(kernel, n_gx, n_gy, n_gz, cap, rows), ou...  29.6 us
    pallas_call x1, Pallas kernels, per_device(): pl.pallas_call(hand_out, out_shape=tuple((jax.ShapeDtypeStruct(result.sha...  1.39 us

profile of v7, /device:TPU:0, one launch (start us, length us, event | category | flops | bytes accessed | tf_op | source)
XLA Modules:
  0.0 31.6 jit_solution(15525246007964340977)
XLA Ops:
  0.6 29.6 %shard_map.156 = (f32[3,8,16,128]{3,2,1,0:T(8,128)S(1)}, f32[3,8,16,128]{3,2,1,0:T(8,128)S(1)}, f32[32,2048]{1,0:T(8,128)S(1)}, f32[8,3,8,16,128]{4,3,2,1,0:T(8,128)S(1)}) custom-call(f32[8]{0:T(128)} %decay_hbm.1, f32[8]{0:T(128)} %gain_hbm.1, f32[3,8,16,128]{3,2,1,0:T(8,128)} %e_hbm.1, f32[3,8,16,128]{3,2,1,0:T(8,128)} %h_hbm.1, f32[8,16,128]{2,1,0:T(8,128)} %perm_hbm.1, ...), custom_call_target="tpu_custom_call" | custom-call | tf_op jit(solution)/shard_map/pallas_call | solution.py:629
  30.2 1.4 %shard_map.157 = (f32[3,8,16,128]{3,2,1,0:T(8,128)}, f32[3,8,16,128]{3,2,1,0:T(8,128)}, f32[8,3,8,16,128]{4,3,2,1,0:T(8,128)}, f32[32,2048]{1,0:T(8,128)}) custom-call(f32[3,8,16,128]{3,2,1,0:T(8,128)S(1)} %get-tuple-element.12.refs_0_, f32[3,8,16,128]{3,2,1,0:T(8,128)S(1)} %get-tuple-element.13.refs_1_, ...), custom_call_target="tpu_custom_call" | custom-call | tf_op jit(solution)/shard_map/pallas_call | solution.py:693
